TPU v7x, 128 devices: a whole 4x4x4 slice. The times are simulated.
128 devices in a mesh: frame: 8 (over z, y_lo), tile: 16 (over x, y_hi, core).
Axes of the slice: x: 4, y: 4 (y_hi: 2, y_lo: 2; y = y_hi * 2 + y_lo), z: 4, core: 2. Of those that a mesh axis runs over, the one named last changes fastest.
Arguments:
- patch_tokens: bfloat16 [32, 1024, 768], P('frame', 'tile'), may hold values from -6 to 6
- gain_time: float32 [768], replicated, may hold values from 0.1 to 1.9
- qkv_time: bfloat16 [768, 2304], replicated, may hold values from -1 to 1
- out_time: bfloat16 [768, 768], replicated, may hold values from -0.21875 to 0.21875
- gain_space: float32 [768], replicated, may hold values from 0.1 to 1.9
- qkv_space: bfloat16 [768, 2304], replicated, may hold values from -1 to 1
- out_space: bfloat16 [768, 768], replicated, may hold values from -0.21875 to 0.21875
- cotangent: bfloat16 [32, 1024, 768], P('frame', 'tile'), may hold values from -6 to 6
Outputs:
- block_output: bfloat16 [32, 1024, 768], P('frame', 'tile')
- input_grad: bfloat16 [32, 1024, 768], P('frame', 'tile')
All inputs are finite; a program needn't handle non-finite values.
Results may differ from a plain program's by a relative error of at most 0.028.
Values may be sent and summed in bfloat16 or wider, within the bound.
No kernel may reach another device: no remote copies, remote signals or barrier semaphores. Data moves between devices by JAX's collectives and lax.ppermute only.
A program may use at most 192 MiB of HBM per device.

v0:
```python
import jax
import jax.numpy as jnp
from jax import lax
from jax.sharding import PartitionSpec as P

HEADS = 12


EPSILON = 1e-05


def split_heads(array):
    return array.reshape(array.shape[:-1] + (HEADS, array.shape[-1] // HEADS))


def join_heads(array):
    return array.reshape(array.shape[:-2] + (array.shape[-2] * array.shape[-1],))


def norm_forward(tokens_in, gain):
    wide = tokens_in.astype(jnp.float32)
    average = jnp.mean(wide, axis=-1, keepdims=True)
    centred = wide - average
    inverse = lax.rsqrt(jnp.mean(centred * centred, axis=-1, keepdims=True) + EPSILON)
    normed = centred * inverse
    return ((normed * gain).astype(jnp.bfloat16), normed, inverse)


def norm_backward(grad_normed, gain, normed, inverse):
    scaled = grad_normed * gain
    return inverse * (
        scaled
        - jnp.mean(scaled, axis=-1, keepdims=True)
        - normed * jnp.mean(scaled * normed, axis=-1, keepdims=True)
    )


def probabilities(queries, key_rows, query_form, key_form):
    scores = jnp.einsum(
        query_form + "," + key_form + "->ahij",
        queries,
        key_rows,
        preferred_element_type=jnp.float32,
    ) * queries.shape[-1] ** (-0.5)
    row_max = jnp.max(scores, axis=-1, keepdims=True)
    lifted = jnp.exp(scores - row_max)
    return lifted / jnp.sum(lifted, axis=-1, keepdims=True)


def attend(queries, key_rows, value_rows, query_form, key_form):
    weights = probabilities(queries, key_rows, query_form, key_form).astype(jnp.bfloat16)
    return jnp.einsum(
        "ahij," + key_form + "->" + query_form,
        weights,
        value_rows,
        preferred_element_type=jnp.float32,
    ).astype(jnp.bfloat16)


def grad_pieces(grad_out, queries, key_rows, value_rows, attended, query_form, key_form):
    weights = probabilities(queries, key_rows, query_form, key_form)
    grad_weights = jnp.einsum(
        query_form + "," + key_form + "->ahij",
        grad_out,
        value_rows,
        preferred_element_type=jnp.float32,
    )
    delta_rows = jnp.einsum(
        query_form + "," + query_form + "->ahi",
        grad_out,
        attended,
        preferred_element_type=jnp.float32,
    )
    grad_scores = (
        weights * (grad_weights - delta_rows[..., None]) * queries.shape[-1] ** (-0.5)
    ).astype(jnp.bfloat16)
    grad_query = jnp.einsum(
        "ahij," + key_form + "->" + query_form,
        grad_scores,
        key_rows,
        preferred_element_type=jnp.float32,
    )
    return (grad_query, grad_scores, weights.astype(jnp.bfloat16))


def sublayer_input_grad(grad_in, grad_qkv, gain, weight_qkv, normed, inverse):
    grad_normed = jnp.einsum(
        "fpc,dc->fpd", grad_qkv, weight_qkv, preferred_element_type=jnp.float32
    )
    return (grad_in.astype(jnp.float32) + norm_backward(grad_normed, gain, normed, inverse)).astype(
        jnp.bfloat16
    )


def local(patch_tokens, gain_time, qkv_time, out_time, gain_space, qkv_space, out_space, cotangent):
    features = patch_tokens.shape[-1]
    normed_half, normed_time, inverse_time = norm_forward(patch_tokens, gain_time)
    projected = jnp.dot(normed_half, qkv_time, preferred_element_type=jnp.float32).astype(
        jnp.bfloat16
    )
    time_query = split_heads(projected[..., :features])
    keys_whole, values_whole = (
        lax.all_gather(projected[..., features : 2 * features], "frame", axis=0, tiled=True),
        lax.all_gather(projected[..., 2 * features :], "frame", axis=0, tiled=True),
    )
    time_keys = split_heads(keys_whole)
    time_values = split_heads(values_whole)
    time_output = attend(time_query, time_keys, time_values, "iahe", "jahe")
    attended_time = join_heads(time_output)
    hidden = (
        patch_tokens.astype(jnp.float32)
        + jnp.dot(attended_time, out_time, preferred_element_type=jnp.float32)
    ).astype(jnp.bfloat16)
    space_half, normed_space, inverse_space = norm_forward(hidden, gain_space)
    space_proj = jnp.dot(space_half, qkv_space, preferred_element_type=jnp.float32).astype(
        jnp.bfloat16
    )
    grad_space_out = split_heads(
        jnp.einsum("fpd,ed->fpe", cotangent, out_space, preferred_element_type=jnp.float32).astype(
            jnp.bfloat16
        )
    )
    space_query = split_heads(space_proj[..., :features])
    space_keys_whole, space_values_whole = (
        lax.all_gather(space_proj[..., features : 2 * features], "tile", axis=1, tiled=True),
        lax.all_gather(space_proj[..., 2 * features :], "tile", axis=1, tiled=True),
    )
    space_keys = split_heads(space_keys_whole)
    space_values = split_heads(space_values_whole)
    space_output = attend(space_query, space_keys, space_values, "aihe", "ajhe")
    block_output = (
        hidden.astype(jnp.float32)
        + jnp.dot(join_heads(space_output), out_space, preferred_element_type=jnp.float32)
    ).astype(jnp.bfloat16)
    grad_query, grad_scores, weights_half = grad_pieces(
        grad_space_out, space_query, space_keys, space_values, space_output, "aihe", "ajhe"
    )
    key_terms = jnp.einsum(
        "ahij,aihe->ajhe", grad_scores, space_query, preferred_element_type=jnp.float32
    )
    value_terms = jnp.einsum(
        "ahij,aihe->ajhe", weights_half, grad_space_out, preferred_element_type=jnp.float32
    )
    key_sum, value_sum = (
        lax.psum_scatter(
            join_heads(key_terms).astype(jnp.bfloat16), "tile", scatter_dimension=1, tiled=True
        ).astype(jnp.float32),
        lax.psum_scatter(
            join_heads(value_terms).astype(jnp.bfloat16), "tile", scatter_dimension=1, tiled=True
        ).astype(jnp.float32),
    )
    grad_space_qkv = jnp.concatenate(
        [
            join_heads(grad_query).astype(jnp.bfloat16),
            key_sum.astype(jnp.bfloat16),
            value_sum.astype(jnp.bfloat16),
        ],
        axis=-1,
    )
    grad_hidden = sublayer_input_grad(
        cotangent, grad_space_qkv, gain_space, qkv_space, normed_space, inverse_space
    )
    grad_time_local = jnp.einsum(
        "fpd,ed->fpe", grad_hidden, out_time, preferred_element_type=jnp.float32
    ).astype(jnp.bfloat16)
    grad_time_out = split_heads(grad_time_local)
    time_grad_query, time_grad_scores, time_weights = grad_pieces(
        grad_time_out, time_query, time_keys, time_values, time_output, "iahe", "jahe"
    )
    time_key_terms = jnp.einsum(
        "ahij,iahe->jahe", time_grad_scores, time_query, preferred_element_type=jnp.float32
    )
    time_value_terms = jnp.einsum(
        "ahij,iahe->jahe", time_weights, grad_time_out, preferred_element_type=jnp.float32
    )
    time_key_sum, time_value_sum = (
        lax.psum_scatter(
            join_heads(time_key_terms).astype(jnp.bfloat16),
            "frame",
            scatter_dimension=0,
            tiled=True,
        ).astype(jnp.float32),
        lax.psum_scatter(
            join_heads(time_value_terms).astype(jnp.bfloat16),
            "frame",
            scatter_dimension=0,
            tiled=True,
        ).astype(jnp.float32),
    )
    grad_time_qkv = jnp.concatenate(
        [
            join_heads(time_grad_query).astype(jnp.bfloat16),
            time_key_sum.astype(jnp.bfloat16),
            time_value_sum.astype(jnp.bfloat16),
        ],
        axis=-1,
    )
    input_grad = sublayer_input_grad(
        grad_hidden, grad_time_qkv, gain_time, qkv_time, normed_time, inverse_time
    )
    return (block_output, input_grad)


def solution(mesh):
    in_specs = (P("frame", "tile", None), P(), P(), P(), P(), P(), P(), P("frame", "tile", None))
    out_specs = (P("frame", "tile", None), P("frame", "tile", None))
    return jax.shard_map(local, mesh=mesh, in_specs=in_specs, out_specs=out_specs, check_vma=False)
```

profile of v0, /device:TPU:0, one launch (start us, length us, event | category | flops | bytes accessed | tf_op | source)
XLA Modules:
  0.0 691.2 jit_solution(9796413355206736858)
XLA Ops:
  9.8 3.3 convolution_convert_fusion.1
  14.9 2.5 reshape.95
  17.4 71.0 %all-gather.7.cloned.1.call-done = bf16[32,64,768]{2,1,0:T(8,128)(2,1)} async-done(((bf16[4,64,768]{2,1,0:T(8,128)(2,1)}), bf16[32,64,768]{2,1,0:T(8,128)(2,1)}) %all-gather.7.cloned.1.call-update) | async-done | bytes 3145744 | tf_op jit(solution)/shard_map/all_gather | solution.py:103
  88.4 10.6 %reshape.96 = bf16[32,64,12,64]{3,2,1,0:T(8,128)(2,1)} reshape(bf16[32,64,768]{2,1,0:T(8,128)(2,1)} %all-gather.7.cloned.1.call-done) | data formatting | bytes 6291456 | tf_op jit(solution)/shard_map/reshape | solution.py:13
  99.0 11.0 %fusion.94 = (f32[64,12,4]{2,1,0:T(8,128)}, f32[64,12,4,32]{3,2,1,0:T(4,128)}) fusion(bf16[32,64,12,64]{3,2,1,0:T(8,128)(2,1)} %reshape.96, bf16[4,64,12,64]{3,2,1,0:T(8,128)(2,1)} %reshape.95), kind=kOutput, calls=%fused_computation.113 | convolution fusion | flops 12877855 | bytes 3944448 | tf_op jit(solution)/shard_map/sub | solution.py:46
  110.0 51.2 %all-gather.5.cloned.1.call-done = bf16[32,64,768]{2,1,0:T(8,128)(2,1)} async-done(((bf16[4,64,768]{2,1,0:T(8,128)(2,1)}), bf16[32,64,768]{2,1,0:T(8,128)(2,1)}) %all-gather.5.cloned.1.call-update) | async-done | bytes 3145744 | tf_op jit(solution)/shard_map/all_gather | solution.py:104
  161.2 10.7 %reshape.94 = bf16[32,64,12,64]{3,2,1,0:T(8,128)(2,1)} reshape(bf16[32,64,768]{2,1,0:T(8,128)(2,1)} %all-gather.5.cloned.1.call-done) | data formatting | bytes 6291456 | tf_op jit(solution)/shard_map/reshape | solution.py:13
  171.9 7.9 %fusion.33 = bf16[64,12,64,4]{2,3,1,0:T(4,128)(2,1)S(1)} fusion(bf16[32,64,12,64]{3,2,1,0:T(8,128)(2,1)} %reshape.94, f32[64,12,4,32]{3,2,1,0:T(4,128)} %get-tuple-element.13, f32[64,12,4]{2,1,0:T(8,128)} %get-tuple-element.12), kind=kOutput, calls=%fused_computation.37 | convolution fusion | flops 12976128 | bytes 3944448 | tf_op jit(solution)/shard_map/ahij,jahe->iahe/dot_general | solution.py:52
  181.8 2.5 reshape.97
  184.3 2.0 fusion.95
  186.6 1.9 convolution_convert_fusion
  190.2 2.6 convolution_convert_fusion.7
  192.8 2.6 reshape.102
  195.5 2.5 copy.63
  198.0 2.2 copy.87
  200.2 53.2 %all-gather.11.cloned.1.call-done = bf16[4,1024,768]{2,1,0:T(8,128)(2,1)} async-done(((bf16[4,64,768]{2,1,0:T(8,128)(2,1)}), bf16[4,1024,768]{2,1,0:T(8,128)(2,1)}) %all-gather.11.cloned.1.call-update) | async-done | bytes 6291472 | tf_op jit(solution)/shard_map/all_gather | solution.py:125
  253.4 8.6 %copy.57 = bf16[4,1024,768]{1,2,0:T(8,128)(2,1)} copy(bf16[4,1024,768]{2,1,0:T(8,128)(2,1)} %all-gather.11.cloned.1.call-done) | data formatting | bytes 12582912 | tf_op jit(solution)/shard_map/all_gather | solution.py:125
  262.0 12.7 %fusion.96 = (f32[4,12,64]{2,1,0:T(8,128)}, f32[4,12,64,1024]{3,2,1,0:T(8,128)}) fusion(bf16[4,64,12,64]{1,3,2,0:T(8,128)(2,1)} %bitcast.88, bf16[4,1024,12,64]{1,3,2,0:T(8,128)(2,1)} %bitcast.82), kind=kOutput, calls=%fused_computation.115 | convolution fusion | flops 412091392 | bytes 19279872 | tf_op jit(solution)/shard_map/sub | solution.py:46
  274.7 5.7 fusion.6
  280.4 4.6 convolution_convert_fusion.2
  285.0 8.5 %copy.64 = bf16[4,1024,768]{2,1,0:T(8,128)(2,1)} copy(bf16[4,1024,768]{1,2,0:T(8,128)(2,1)} %bitcast.87) | data formatting | bytes 12582912 | tf_op jit(solution)/shard_map/convert_element_type | solution.py:149
  293.5 2.7 bitcast_convert_fusion.1
  296.3 3.0 copy.80
  299.3 19.1 %all-gather.9.cloned.1.call-done = bf16[4,1024,768]{2,1,0:T(8,128)(2,1)} async-done(((bf16[4,64,768]{2,1,0:T(8,128)(2,1)}), bf16[4,1024,768]{2,1,0:T(8,128)(2,1)}) %all-gather.9.cloned.1.call-update) | async-done | bytes 6291472 | tf_op jit(solution)/shard_map/all_gather | solution.py:126
  318.4 8.7 %copy.56 = bf16[4,1024,768]{1,2,0:T(8,128)(2,1)} copy(bf16[4,1024,768]{2,1,0:T(8,128)(2,1)} %all-gather.9.cloned.1.call-done) | data formatting | bytes 12582912 | tf_op jit(solution)/shard_map/all_gather | solution.py:126
  327.0 8.6 %multiply_reduce_fusion.2 = (f32[4,12,64]{2,1,0:T(8,128)S(1)}, bf16[4,12,64,64]{3,2,1,0:T(8,128)(2,1)}) fusion(f32[4,12,64,64]{2,3,1,0:T(8,128)} %copy.80, bf16[4,1024,12,64]{1,3,2,0:T(8,128)(2,1)} %bitcast.84, bf16[4,12,64,1024]{3,2,1,0:T(8,128)(2,1)} %copy-done.1), kind=kOutput, calls=%fused_computation.32 | convolution fusion | flops 403436544 | bytes 13774848 | tf_op jit(solution)/shard_map/ahij,ajhe->aihe/dot_general | solution.py:52
  335.7 7.1 %multiply_convert_fusion = bf16[4,12,64,1024]{3,2,1,0:T(8,128)(2,1)S(1)} fusion(f32[4,12,64]{2,1,0:T(8,128)S(1)} %get-tuple-element.18, f32[4,12,64,1024]{3,2,1,0:T(8,128)} %get-tuple-element.17, f32[4,12,64]{2,1,0:T(8,128)S(1)} %copy-done.19, bf16[4,64,12,64]{1,3,2,0:T(8,128)(2,1)S(1)} %copy-done.14, bf16[4,1024,12,64]{1,3,2,0:T(8,128)(2,1)S(1)} %bitcast.85), kind=kOutput, calls=%fused_computation.2 | convolution fusion | flops 418381824 | bytes 25583616 | tf_op jit(solution)/shard_map/aihe,ajhe->ahij/dot_general | solution.py:62
  342.8 4.6 convolution_convert_fusion.3
  347.5 8.7 %copy.62 = bf16[4,1024,768]{2,1,0:T(8,128)(2,1)} copy(bf16[4,1024,768]{1,2,0:T(8,128)(2,1)} %bitcast.86) | data formatting | bytes 12582912 | tf_op jit(solution)/shard_map/convert_element_type | solution.py:146
  356.2 7.6 %convolution_convert_fusion.4 = bf16[4,12,64,64]{3,2,1,0:T(8,128)(2,1)} fusion(bf16[4,1024,12,64]{1,3,2,0:T(8,128)(2,1)} %bitcast.83, bf16[4,12,64,1024]{3,2,1,0:T(8,128)(2,1)} %copy-done.2), kind=kOutput, calls=%fused_computation.38 | convolution fusion | flops 402849792 | bytes 12976128 | tf_op jit(solution)/shard_map/ahij,ajhe->aihe/dot_general | solution.py:77
  363.8 2.1 copy.65
  365.9 44.5 %reduce-scatter.7.cloned.1.call-done = bf16[4,64,768]{2,1,0:T(8,128)(2,1)} async-done(((bf16[4,1024,768]{2,1,0:T(8,128)(2,1)}), bf16[4,64,768]{2,1,0:T(8,128)(2,1)}) %reduce-scatter.7.cloned.1.call-update) | async-done | bytes 393232 | tf_op jit(solution)/shard_map/reduce_scatter | solution.py:148
  410.4 92.4 %reduce-scatter.5.cloned.1.call-done = bf16[4,64,768]{2,1,0:T(8,128)(2,1)} async-done(((bf16[4,1024,768]{2,1,0:T(8,128)(2,1)}), bf16[4,64,768]{2,1,0:T(8,128)(2,1)}) %reduce-scatter.5.cloned.1.call-update) | async-done | bytes 393232 | tf_op jit(solution)/shard_map/reduce_scatter | solution.py:145
  502.9 2.9 fusion.91
  508.1 2.9 reshape.103
  510.9 6.3 convert_bitcast_fusion
  517.2 5.9 copy.73
  523.2 11.2 %convert_element_type.170 = bf16[32,64,768]{2,1,0:T(8,128)(2,1)} reshape(bf16[32,64,12,64]{3,2,1,0:T(8,128)(2,1)} %copy.73) | data formatting | bytes 6291456 | tf_op jit(solution)/shard_map/convert_element_type | solution.py:184
  537.3 8.3 %multiply_convert_fusion.1 = bf16[64,12,4,32]{3,2,1,0:T(4,128)(2,1)S(1)} fusion(bf16[32,64,12,64]{3,2,1,0:T(8,128)(2,1)} %reshape.94, f32[64,12,4]{2,1,0:T(8,128)S(1)} %multiply_reduce_fusion.1, bf16[4,64,12,64]{3,2,1,0:T(8,128)(2,1)S(1)} %copy-done.9, f32[64,12,4,32]{3,2,1,0:T(4,128)S(1)} %copy-done.21, f32[64,12,4]{2,1,0:T(8,128)S(1)} %copy-done.22), kind=kOutput, calls=%fused_computation.33 | convolution fusion | flops 13074432 | bytes 4153344 | tf_op jit(solution)/shard_map/iahe,jahe->ahij/dot_general | solution.py:62
  546.5 2.3 convert_bitcast_fusion.1
  548.9 5.9 copy.71
  554.8 11.2 %convert_element_type.167 = bf16[32,64,768]{2,1,0:T(8,128)(2,1)} reshape(bf16[32,64,12,64]{3,2,1,0:T(8,128)(2,1)} %copy.71) | data formatting | bytes 6291456 | tf_op jit(solution)/shard_map/convert_element_type | solution.py:178
  566.0 3.0 fusion.47
  569.0 7.4 %fusion.36 = bf16[4,64,12,64]{3,0,2,1:T(4,128)(2,1)S(1)} fusion(bf16[64,12,4,32]{3,2,1,0:T(4,128)(2,1)} %copy-done.18, bf16[32,64,12,64]{3,2,1,0:T(8,128)(2,1)} %reshape.96), kind=kOutput, calls=%fused_computation.41 | convolution fusion | flops 12779520 | bytes 3735552 | tf_op jit(solution)/shard_map/ahij,jahe->iahe/dot_general | solution.py:77
  577.5 2.5 convert_element_type.164
  580.0 25.3 %reduce-scatter.11.cloned.1.call-done = bf16[4,64,768]{2,1,0:T(8,128)(2,1)} async-done(((bf16[32,64,768]{2,1,0:T(8,128)(2,1)}), bf16[4,64,768]{2,1,0:T(8,128)(2,1)}) %reduce-scatter.11.cloned.1.call-update) | async-done | bytes 393232 | tf_op jit(solution)/shard_map/reduce_scatter | solution.py:183
  605.4 74.0 %reduce-scatter.9.cloned.1.call-done = bf16[4,64,768]{2,1,0:T(8,128)(2,1)} async-done(((bf16[32,64,768]{2,1,0:T(8,128)(2,1)}), bf16[4,64,768]{2,1,0:T(8,128)(2,1)}) %reduce-scatter.9.cloned.1.call-update) | async-done | bytes 393232 | tf_op jit(solution)/shard_map/reduce_scatter | solution.py:177
  679.4 3.7 fusion.90
  (81 shorter events, 16.8 us)
Async XLA Ops:
  7.2 179.5 %copy-start = (bf16[768,2304]{1,0:T(8,128)(2,1)S(1)}, bf16[768,2304]{1,0:T(8,128)(2,1)}, u32[]{:S(2)}) copy-start(bf16[768,2304]{1,0:T(8,128)(2,1)} %param.13) | copy-start | bytes 10616836
  7.2 81.2 %all-gather.7.cloned.1.call-start = ((), (), s32[]{:S(2)}) async-start(), calls=%async_computation.5 | async-start | bytes 3538944 | tf_op jit(solution)/shard_map/all_gather | solution.py:103
  14.1 147.0 %all-gather.5.cloned.1.call-start = ((), (), s32[]{:S(2)}) async-start(), calls=%async_computation.4 | async-start | bytes 3538944 | tf_op jit(solution)/shard_map/all_gather | solution.py:104
  14.9 238.5 %all-gather.11.cloned.1.call-start = ((), (), s32[]{:S(2)}) async-start(), calls=%async_computation.7 | async-start | bytes 6684672 | tf_op jit(solution)/shard_map/all_gather | solution.py:125
  179.8 0.9 copy-start.15
  186.4 3.2 copy-start.4
  189.6 128.8 %all-gather.9.cloned.1.call-start = ((), (), s32[]{:S(2)}) async-start(), calls=%async_computation.6 | async-start | bytes 6684672 | tf_op jit(solution)/shard_map/all_gather | solution.py:126
  190.1 220.3 %reduce-scatter.7.cloned.1.call-start = ((), (), s32[]{:S(2)}) async-start(), calls=%async_computation.9 | async-start | bytes 6684672 | tf_op jit(solution)/shard_map/reduce_scatter | solution.py:148
  274.7 5.7 copy-start.13
  280.4 4.6 copy-start.1
  293.5 209.4 %reduce-scatter.5.cloned.1.call-start = ((), (), s32[]{:S(2)}) async-start(), calls=%async_computation.8 | async-start | bytes 6684672 | tf_op jit(solution)/shard_map/reduce_scatter | solution.py:145
  327.0 8.6 %copy-start.3 = (bf16[4,1024,768]{1,2,0:T(8,128)(2,1)S(1)}, bf16[4,1024,768]{1,2,0:T(8,128)(2,1)}, u32[]{:S(2)}) copy-start(bf16[4,1024,768]{1,2,0:T(8,128)(2,1)} %copy.56) | copy-start | bytes 18874372
  327.0 8.6 %copy-start.14 = (bf16[4,64,12,64]{1,3,2,0:T(8,128)(2,1)S(1)}, bf16[4,64,12,64]{1,3,2,0:T(8,128)(2,1)}, u32[]{:S(2)}) copy-start(bf16[4,64,12,64]{1,3,2,0:T(8,128)(2,1)} %copy.63) | copy-start | bytes 1179652
  327.0 8.6 %copy-start.19 = (f32[4,12,64]{2,1,0:T(8,128)S(1)}, f32[4,12,64]{2,1,0:T(8,128)}, u32[]{:S(2)}) copy-start(f32[4,12,64]{2,1,0:T(8,128)} %get-tuple-element.16) | copy-start | bytes 36868
  335.7 7.1 %copy-start.6 = (bf16[4,64,768]{1,2,0:T(8,128)(2,1)S(1)}, bf16[4,64,768]{1,2,0:T(8,128)(2,1)}, u32[]{:S(2)}) copy-start(bf16[4,64,768]{1,2,0:T(8,128)(2,1)} %copy.87) | copy-start | bytes 1179652
  342.8 4.7 copy-start.2
  356.1 249.2 %reduce-scatter.11.cloned.1.call-start = ((), (), s32[]{:S(2)}) async-start(), calls=%async_computation.11 | async-start | bytes 3538944 | tf_op jit(solution)/shard_map/reduce_scatter | solution.py:183
  502.9 2.9 copy-start.5
  502.9 2.9 copy-start.17
  502.9 3.9 copy-start.8
  506.1 0.7 copy-start.10
  534.3 145.0 %reduce-scatter.9.cloned.1.call-start = ((), (), s32[]{:S(2)}) async-start(), calls=%async_computation.10 | async-start | bytes 3538944 | tf_op jit(solution)/shard_map/reduce_scatter | solution.py:177
  534.4 1.6 copy-start.16
  534.4 2.9 copy-start.9
  534.4 2.9 copy-start.21
  534.4 2.9 copy-start.22
  537.3 9.2 %copy-start.12 = (bf16[4,64,12,64]{3,2,1,0:T(8,128)(2,1)S(1)}, bf16[4,64,12,64]{3,2,1,0:T(8,128)(2,1)}, u32[]{:S(2)}) copy-start(bf16[4,64,12,64]{3,2,1,0:T(8,128)(2,1)} %reshape.95) | copy-start | bytes 1179652
  545.6 0.9 copy-start.18
  569.0 110.4 %copy-start.20 = (f32[768]{0:T(1024)S(1)}, f32[768]{0:T(1024)}, u32[]{:S(2)}) copy-start(f32[768]{0:T(1024)} %param.9) | copy-start | bytes 9220
  679.4 3.8 copy-start.7
  679.4 3.8 copy-start.11
Sparse Core Ops, SparseCore 0:
  14.2 74.0 all-gather.6
  90.0 71.0 all-gather.4
  189.7 63.6 all-gather.10
  255.7 62.6 all-gather.8
  322.3 88.0 reduce-scatter.6
  414.4 88.3 reduce-scatter.4
  534.5 70.8 reduce-scatter.10
  607.8 71.5 reduce-scatter.8
where the time goes:
time: 701 us; the launch traced here: 691 us
  waiting for transfers between devices  432 us (62%)
  local copies, waits for them, and re-layouts  120 us (17%)
  matrix products  109 us (16%)
  other arithmetic  15.4 us (2%)
  between operations  14.7 us (2%)
    reduce_scatter x1, waiting for transfers between devices, local(): lax.psum_scatter(join_heads(key_terms).astype(jnp.bfloat16), 'tile', scat...  92.4 us
    reduce_scatter x1, waiting for transfers between devices, local(): lax.psum_scatter(join_heads(time_key_terms).astype(jnp.bfloat16), 'frame'...  74 us
    all_gather x1, waiting for transfers between devices, local(): lax.all_gather(projected[..., features:2 * features], 'frame', axis=0, ti...  71 us
    all_gather x1, waiting for transfers between devices, local(): lax.all_gather(space_proj[..., features:2 * features], 'tile', axis=1, ti...  53.2 us
    all_gather x1, waiting for transfers between devices, local(): lax.all_gather(projected[..., 2 * features:], 'frame', axis=0, tiled=True)  51.2 us
    reduce_scatter x1, waiting for transfers between devices, local(): lax.psum_scatter(join_heads(value_terms).astype(jnp.bfloat16), 'tile', sc...  44.5 us
    reshape x7, local copies, waits for them, and re-layouts, split_heads(): return array.reshape(array.shape[:-1] + (HEADS, array.shape[-1] // HEADS))  34 us
    reduce_scatter x1, waiting for transfers between devices, local(): lax.psum_scatter(join_heads(time_value_terms).astype(jnp.bfloat16), 'fram...  25.3 us
  transfers between devices with their start and end apart: 8, of which 8 were waited for; matrix products, arithmetic and copies ran while one was open for 25% of the time, Pallas kernels for 0%

commit v1 on v0

v1 whole, which is shorter than its diff:
```python
import functools

import jax
import jax.numpy as jnp
from jax import lax
from jax.experimental import pallas as pl
from jax.experimental.pallas import tpu as pltpu
from jax.sharding import PartitionSpec as P

HEADS = 12
EPSILON = 1e-05
F32 = jnp.float32
BF16 = jnp.bfloat16
VMEM = pl.BlockSpec(memory_space=pltpu.VMEM)
ANY = pl.BlockSpec(memory_space=pl.ANY)
LIMIT = 56 * 1024 * 1024


def dot(a, b):
    return jnp.dot(a, b, preferred_element_type=F32)


def dot_last(a, b):
    return lax.dot_general(a, b, (((1,), (1,)), ((), ())), preferred_element_type=F32)


def norm_stats(wide):
    average = jnp.mean(wide, axis=-1, keepdims=True)
    centred = wide - average
    inverse = lax.rsqrt(jnp.mean(centred * centred, axis=-1, keepdims=True) + EPSILON)
    return centred * inverse, inverse


def norm_backward(grad_normed, gain, normed, inverse):
    scaled = grad_normed * gain
    return inverse * (
        scaled
        - jnp.mean(scaled, axis=-1, keepdims=True)
        - normed * jnp.mean(scaled * normed, axis=-1, keepdims=True)
    )


def same_patch(tokens, patches):
    rows = lax.broadcasted_iota(jnp.int32, (tokens, tokens), 0)
    columns = lax.broadcasted_iota(jnp.int32, (tokens, tokens), 1)
    return (rows % patches) == (columns % patches)


def time_forward_kernel(
    patches, groups,
    both_ref, gain_time_ref, gain_space_ref, qkv_time_hbm, out_time_hbm, qkv_space_hbm, out_space_hbm,
    send_ref, hidden_ref, qkv_ref, attended_ref, prob_ref,
    qkv_time_ref, out_time_ref, qkv_space_ref, out_space_ref, sems,
):
    copies = [
        pltpu.make_async_copy(src, dst, sems.at[n])
        for n, (src, dst) in enumerate((
            (qkv_time_hbm, qkv_time_ref), (out_space_hbm, out_space_ref),
            (out_time_hbm, out_time_ref), (qkv_space_hbm, qkv_space_ref),
        ))
    ]
    for copy in copies:
        copy.start()
    tokens, features = hidden_ref.shape
    size = features // HEADS
    part = features // groups
    tokens_in = both_ref[:, 0].reshape(tokens, features).astype(F32)
    cotangent = both_ref[:, 1].reshape(tokens, features)
    normed, _ = norm_stats(tokens_in)
    normed_half = (normed * gain_time_ref[...]).astype(BF16)
    copies[0].wait()
    qkv = dot(normed_half, qkv_time_ref[...]).astype(BF16)
    qkv_ref[...] = qkv
    copies[1].wait()
    grad_out = dot_last(cotangent, out_space_ref[...]).astype(BF16)
    qkv_t = qkv.T
    mask = same_patch(tokens, patches)
    outputs = []
    for h in range(HEADS):
        keys = qkv[:, features + h * size : features + (h + 1) * size]
        queries_t = qkv_t[h * size : (h + 1) * size] * jnp.asarray(size ** -0.5, BF16)
        scores = jnp.where(mask, dot(keys, queries_t), -1e30)
        lifted = jnp.exp(scores - jnp.max(scores, axis=0, keepdims=True))
        prob = (lifted / jnp.sum(lifted, axis=0, keepdims=True)).astype(BF16)
        prob_ref[h] = prob
        values_t = qkv_t[2 * features + h * size : 2 * features + (h + 1) * size]
        outputs.append(dot(values_t, prob))
    attended = jnp.concatenate(outputs, axis=0).T.astype(BF16)
    attended_ref[...] = attended
    copies[2].wait()
    hidden = (tokens_in + dot(attended, out_time_ref[...])).astype(BF16)
    hidden_ref[...] = hidden
    normed_space, _ = norm_stats(hidden.astype(F32))
    space_half = (normed_space * gain_space_ref[...]).astype(BF16)
    copies[3].wait()
    space = dot(space_half, qkv_space_ref[...]).astype(BF16)
    for g in range(groups):
        send_ref[g] = jnp.concatenate(
            [space[:, n * features + g * part : n * features + (g + 1) * part] for n in range(3)]
            + [grad_out[:, g * part : (g + 1) * part]],
            axis=1,
        )


def space_kernel(heads, block, got_ref, back_ref, nat, tra, out_t, grad_t, grad_key, grad_value):
    tokens, width = got_ref.shape
    part = width // 4
    size = part // heads
    scale = size ** -0.5
    got = got_ref[...]
    got_t = got.T
    for n in range(4):
        for h in range(heads):
            at = n * part + h * size
            nat[n, h] = got[:, at : at + size]
            piece = got_t[at : at + size]
            tra[n, h] = piece * jnp.asarray(scale, BF16) if n == 0 else piece
    blocks = tokens // block

    def step(t, carry):
        h = t // blocks
        b = t % blocks
        at = pl.multiple_of(b * block, block)
        here = pl.ds(at, block)
        scores = dot(nat[1, h], tra[0, h, :, here])
        lifted = jnp.exp(scores - jnp.max(scores, axis=0, keepdims=True))
        prob = lifted * (1.0 / jnp.sum(lifted, axis=0, keepdims=True))
        prob_half = prob.astype(BF16)
        attended_t = dot(tra[2, h], prob_half).astype(BF16)
        out_t[h, :, here] = attended_t
        grad_out_t = tra[3, h, :, here]
        delta = jnp.sum(grad_out_t.astype(F32) * attended_t.astype(F32), axis=0, keepdims=True)
        grad_prob = dot(nat[2, h], grad_out_t)
        grad_scores = (prob * (grad_prob - delta)).astype(BF16)
        grad_t[h, :, here] = dot(tra[1, h], grad_scores) * scale
        key_terms = dot(grad_scores, nat[0, h, here, :])
        value_terms = dot(prob_half, nat[3, h, here, :])

        @pl.when(b == 0)
        def _():
            grad_key[h] = key_terms
            grad_value[h] = value_terms

        @pl.when(b > 0)
        def _():
            grad_key[h] += key_terms
            grad_value[h] += value_terms

        return carry

    lax.fori_loop(0, heads * blocks, step, 0)
    back_ref[:, :part * 2] = jnp.concatenate(
        [out_t[h].astype(F32) for h in range(heads)] + [grad_t[h] for h in range(heads)], axis=0
    ).T.astype(BF16)
    back_ref[:, part * 2:] = jnp.concatenate(
        [grad_key[h] * scale for h in range(heads)] + [grad_value[h] for h in range(heads)], axis=1
    ).astype(BF16)


def time_backward_kernel(
    both_ref, back_ref, hidden_ref, qkv_ref, attended_ref, prob_ref, gain_time_ref, gain_space_ref,
    qkv_time_hbm, out_time_hbm, qkv_space_hbm, out_space_hbm,
    out_ref,
    qkv_time_ref, out_time_ref, qkv_space_ref, out_space_ref, sems,
):
    copies = [
        pltpu.make_async_copy(src, dst, sems.at[n])
        for n, (src, dst) in enumerate((
            (out_space_hbm, out_space_ref), (qkv_space_hbm, qkv_space_ref),
            (out_time_hbm, out_time_ref), (qkv_time_hbm, qkv_time_ref),
        ))
    ]
    for copy in copies:
        copy.start()
    tokens, features = hidden_ref.shape
    groups = back_ref.shape[0]
    part = features // groups
    size = features // HEADS
    scale = size ** -0.5
    shape = (both_ref.shape[0],) + both_ref.shape[2:]

    def column(n):
        return jnp.concatenate(
            [back_ref[g, :, n * part : (n + 1) * part] for g in range(groups)], axis=1
        )

    hidden = hidden_ref[...].astype(F32)
    copies[0].wait()
    block_output = (hidden + dot(column(0), out_space_ref[...])).astype(BF16)
    out_ref[:, 0] = block_output.reshape(shape)
    grad_qkv = jnp.concatenate([column(1), column(2), column(3)], axis=1)
    copies[1].wait()
    grad_normed = dot_last(grad_qkv, qkv_space_ref[...])
    normed, inverse = norm_stats(hidden)
    cotangent = both_ref[:, 1].reshape(tokens, features).astype(F32)
    grad_hidden = (
        cotangent + norm_backward(grad_normed, gain_space_ref[...], normed, inverse)
    ).astype(BF16)
    copies[2].wait()
    grad_out = dot_last(grad_hidden, out_time_ref[...]).astype(BF16)
    qkv = qkv_ref[...]
    keys_t = qkv[:, features : 2 * features].T
    grad_out_t = grad_out.T
    product_t = (grad_out.astype(F32) * attended_ref[...].astype(F32)).T
    queries_grad, keys_grad, values_grad = [], [], []
    for h in range(HEADS):
        own = slice(h * size, (h + 1) * size)
        delta = jnp.sum(product_t[own], axis=0, keepdims=True)
        prob = prob_ref[h]
        values = qkv[:, 2 * features + h * size : 2 * features + (h + 1) * size]
        grad_prob = dot(values, grad_out_t[own])
        grad_scores = (prob.astype(F32) * (grad_prob - delta)).astype(BF16)
        queries_grad.append(dot(keys_t[own], grad_scores) * scale)
        keys_grad.append(dot(grad_scores, qkv[:, own]) * scale)
        values_grad.append(dot(prob, grad_out[:, own]))
    grad_qkv_time = jnp.concatenate(
        [
            jnp.concatenate(queries_grad, axis=0).T.astype(BF16),
            jnp.concatenate(keys_grad, axis=1).astype(BF16),
            jnp.concatenate(values_grad, axis=1).astype(BF16),
        ],
        axis=1,
    )
    copies[3].wait()
    grad_normed_time = dot_last(grad_qkv_time, qkv_time_ref[...])
    tokens_in = both_ref[:, 0].reshape(tokens, features).astype(F32)
    normed_time, inverse_time = norm_stats(tokens_in)
    input_grad = grad_hidden.astype(F32) + norm_backward(
        grad_normed_time, gain_time_ref[...], normed_time, inverse_time
    )
    out_ref[:, 1] = input_grad.astype(BF16).reshape(shape)


def local(
    frame_count, tile_count,
    patch_tokens, gain_time, qkv_time, out_time, gain_space, qkv_space, out_space, cotangent,
):
    frames, patches, features = patch_tokens.shape
    devices = frame_count * tile_count
    own_patches = patches // frame_count
    all_frames = frames * frame_count
    tokens = all_frames * own_patches
    groups = devices // all_frames
    heads = HEADS // groups
    part = features // groups
    params = pltpu.CompilerParams(vmem_limit_bytes=LIMIT)
    gain_time, gain_space = gain_time[None], gain_space[None]
    weights = (qkv_time, out_time, qkv_space, out_space)

    def shaped(shape, dtype=BF16):
        return jax.ShapeDtypeStruct(shape, dtype)

    both = jnp.stack([patch_tokens, cotangent])
    both = both.reshape(2, frames, frame_count, own_patches, features).transpose(2, 0, 1, 3, 4)
    both = lax.all_to_all(both, "frame", 0, 0)
    both = both.reshape(frame_count, 2, frames * own_patches, features)

    weight_scratch = [pltpu.VMEM(w.shape, w.dtype) for w in weights] + [pltpu.SemaphoreType.DMA((4,))]
    send, hidden, qkv, attended, prob = pl.pallas_call(
        functools.partial(time_forward_kernel, own_patches, groups),
        out_shape=(
            shaped((groups, tokens, 4 * part)),
            shaped((tokens, features)),
            shaped((tokens, 3 * features)),
            shaped((tokens, features)),
            shaped((HEADS, tokens, tokens)),
        ),
        in_specs=[VMEM] * 3 + [ANY] * 4,
        out_specs=[VMEM] * 5,
        scratch_shapes=weight_scratch,
        compiler_params=params,
        name="time_forward",
    )(both, gain_time, gain_space, *weights)

    got = lax.all_to_all(
        send.reshape(devices, own_patches, 4 * part), ("frame", "tile"), 0, 0
    ).reshape(devices * own_patches, 4 * part)

    rows = devices * own_patches
    size = features // HEADS
    back = pl.pallas_call(
        functools.partial(space_kernel, heads, 256),
        out_shape=shaped((rows, 4 * part)),
        in_specs=[VMEM],
        out_specs=VMEM,
        scratch_shapes=[
            pltpu.VMEM((4, heads, rows, size), BF16),
            pltpu.VMEM((4, heads, size, rows), BF16),
            pltpu.VMEM((heads, size, rows), BF16),
            pltpu.VMEM((heads, size, rows), F32),
            pltpu.VMEM((heads, rows, size), F32),
            pltpu.VMEM((heads, rows, size), F32),
        ],
        compiler_params=params,
        name="space_attention",
    )(got)

    back = lax.all_to_all(
        back.reshape(devices, own_patches, 4 * part), ("frame", "tile"), 0, 0
    ).reshape(groups, tokens, 4 * part)

    result = pl.pallas_call(
        time_backward_kernel,
        out_shape=shaped(both.shape),
        in_specs=[VMEM] * 8 + [ANY] * 4,
        out_specs=VMEM,
        scratch_shapes=weight_scratch,
        compiler_params=params,
        name="time_backward",
    )(both, back, hidden, qkv, attended, prob, gain_time, gain_space, *weights)

    result = lax.all_to_all(result, "frame", 0, 0)
    result = result.reshape(frame_count, 2, frames, own_patches, features).transpose(1, 2, 0, 3, 4)
    result = result.reshape(2, frames, patches, features)
    return result[0], result[1]


def solution(mesh):
    in_specs = (P("frame", "tile", None), P(), P(), P(), P(), P(), P(), P("frame", "tile", None))
    out_specs = (P("frame", "tile", None), P("frame", "tile", None))
    return jax.shard_map(
        functools.partial(local, mesh.shape["frame"], mesh.shape["tile"]),
        mesh=mesh, in_specs=in_specs, out_specs=out_specs, check_vma=False,
    )
```

time: 701 us -> 152 us (0.22); the launches traced: 691 us -> 152 us
  waiting for transfers between devices: 432 us -> 11.7 us
  local copies, waits for them, and re-layouts: 120 us -> 3.07 us
  matrix products: 109 us -> 0 us
  blocking collectives: 0 us -> 78.3 us
  Pallas kernels: 0 us -> 49.5 us
  between operations: 14.7 us -> 0.68 us
  other arithmetic: 15.4 us -> 2.09 us
    reduce_scatter x4 -> x0, waiting for transfers between devices: 236 us -> none  [the longest x1 92.4 us: local(): lax.psum_scatter(join_heads(key_terms).astype(jnp.bfloat16), 'tile', scat...]
    all_gather x4 -> x0, waiting for transfers between devices: 194 us -> none  [the longest x1 71 us: local(): lax.all_gather(projected[..., features:2 * features], 'frame', axis=0, ti...]
    dot_general x18 -> x0, matrix products: 85.4 us -> none  [the longest x2 16.6 us: attend(): jnp.einsum('ahij,' + key_form + '->' + query_form, weights, value_rows, p...]
    all_to_all x0 -> x3, blocking collectives: none -> 78.3 us  [the longest x1 32.1 us: local(): lax.all_to_all(send.reshape(devices, own_patches, 4 * part), ('frame', 't...]
    convert_element_type x10 -> x0, local copies, waits for them, and re-layouts: 58.3 us -> none  [the longest x2 17.1 us: local(): join_heads(time_key_terms).astype(jnp.bfloat16)]
    pallas_call x0 -> x3, Pallas kernels: none -> 49.5 us  [the longest x1 24.9 us: local(): pl.pallas_call(functools.partial(space_kernel, heads, 256), out_shape=sha...]
    reshape x8 -> x0, local copies, waits for them, and re-layouts: 36.5 us -> none  [the longest x7 34 us: split_heads(): return array.reshape(array.shape[:-1] + (HEADS, array.shape[-1] // HEADS))]
    sub x2 -> x0, matrix products: 23.7 us -> none  [probabilities(): lifted = jnp.exp(scores - row_max)]
  transfers between devices with their start and end apart: 8 -> 1, of which waited for: 8 -> 1; matrix products, arithmetic and copies ran while one was open for 25% -> 1% of each run, Pallas kernels for 0% -> 0%
where the time goes in v1:
time: 152 us
  blocking collectives  78.3 us (52%)
  Pallas kernels  49.5 us (33%)
  waiting for transfers between devices  11.7 us (8%)
  starting transfers between devices  6.41 us (4%)
  local copies, waits for them, and re-layouts  3.07 us (2%)
  other arithmetic  2.09 us (1%)
    all_to_all x1, blocking collectives, local(): lax.all_to_all(send.reshape(devices, own_patches, 4 * part), ('frame', 't...  32.1 us
    all_to_all x1, blocking collectives, local(): lax.all_to_all(back.reshape(devices, own_patches, 4 * part), ('frame', 't...  30 us
    pallas_call x1, Pallas kernels, local(): pl.pallas_call(functools.partial(space_kernel, heads, 256), out_shape=sha...  24.9 us
    all_to_all x1, blocking collectives, local(): result = lax.all_to_all(result, 'frame', 0, 0)  16.2 us
    pallas_call x1, Pallas kernels, local(): pl.pallas_call(time_backward_kernel, out_shape=shaped(both.shape), in_spe...  12.9 us
    pallas_call x1, Pallas kernels, local(): pl.pallas_call(functools.partial(time_forward_kernel, own_patches, groups...  11.8 us
    all_to_all x1, waiting for transfers between devices, local(): both = lax.all_to_all(both, 'frame', 0, 0)  11.7 us
    all_to_all x1, starting transfers between devices, local(): both = lax.all_to_all(both, 'frame', 0, 0)  6.41 us
  transfers between devices with their start and end apart: 1, of which 1 were waited for; matrix products, arithmetic and copies ran while one was open for 1% of the time, Pallas kernels for 0%

profile of v1, /device:TPU:0, one launch (start us, length us, event | category | flops | bytes accessed | tf_op | source)
XLA Modules:
  0.0 151.8 jit_solution(4235826632222319683)
XLA Ops:
  0.6 0.0 copy-start.1
  0.6 0.0 copy-start.2
  0.7 2.1 %copy_bitcast_fusion = bf16[8,2,4,8,768]{4,3,2,1,0:T(8,128)(2,1)} fusion(bf16[1,4,8,8,768]{4,3,2,1,0:T(8,128)(2,1)} %bitcast.23, bf16[1,4,8,8,768]{4,3,2,1,0:T(8,128)(2,1)} %bitcast.24), kind=kLoop, calls=%fused_computation.1 | loop fusion | flops 393216 | bytes 1572864 | tf_op jit(solution)/shard_map/transpose | solution.py:254
  2.7 6.4 %all-to-all-start = ((bf16[8,2,4,8,768]{4,3,2,1,0:T(8,128)(2,1)}), bf16[8,2,4,8,768]{4,3,2,1,0:T(8,128)(2,1)S(1)}, u32[]{:S(2)}, u32[]{:S(2)}) async-start(bf16[8,2,4,8,768]{4,3,2,1,0:T(8,128)(2,1)} %copy_bitcast_fusion), calls=%async_computation | async-start | bytes 1572864 | tf_op jit(solution)/shard_map/all_to_all | solution.py:255
  9.1 0.0 copy-done.1
  9.2 0.6 broadcast_in_dim.6.gain_time_ref
  9.7 0.0 copy-done.2
  9.8 0.6 broadcast_in_dim.7.gain_space_ref
  10.3 11.7 %all-to-all-done = bf16[8,2,4,8,768]{4,3,2,1,0:T(8,128)(2,1)S(1)} async-done(((bf16[8,2,4,8,768]{4,3,2,1,0:T(8,128)(2,1)}), bf16[8,2,4,8,768]{4,3,2,1,0:T(8,128)(2,1)S(1)}, u32[]{:S(2)}, u32[]{:S(2)}) %all-to-all-start) | async-done | bytes 786464 | tf_op jit(solution)/shard_map/all_to_all | solution.py:255
  22.0 0.0 copy-start
  22.0 0.9 copy-done
  22.9 11.8 %time_forward.1 = (bf16[4,256,768]{2,1,0:T(8,128)(2,1)}, bf16[256,768]{1,0:T(8,128)(2,1)}, bf16[256,2304]{1,0:T(8,128)(2,1)}, bf16[256,768]{1,0:T(8,128)(2,1)}, bf16[12,256,256]{2,1,0:T(8,128)(2,1)}) custom-call(bf16[8,2,32,768]{3,2,1,0:T(8,128)(2,1)} %bitcast.16, f32[1,768]{1,0:T(1,128)} %broadcast_in_dim.6.gain_time_ref, ...), custom_call_target="tpu_custom_call" | custom-call | tf_op jit(solution)/shard_map/time_forward/pallas_call | solution.py:259
  34.8 32.1 %all_to_all.20 = bf16[128,8,768]{2,1,0:T(8,128)(2,1)} all-to-all(bf16[128,8,768]{2,1,0:T(8,128)(2,1)} %bitcast.22), channel_id=1, replica_groups=mesh['frame'=8,'tile'=16] {'frame','tile'}, dimensions={0} | all-to-all | bytes 3145728 | tf_op jit(solution)/shard_map/all_to_all | solution.py:275
  66.9 24.9 %space_attention.1 = bf16[1024,768]{1,0:T(8,128)(2,1)} custom-call(bf16[1024,768]{1,0:T(8,128)(2,1)} %bitcast.19), custom_call_target="tpu_custom_call" | custom-call | tf_op jit(solution)/shard_map/space_attention/pallas_call | solution.py:281
  91.8 30.0 %all_to_all.21 = bf16[128,8,768]{2,1,0:T(8,128)(2,1)} all-to-all(bf16[128,8,768]{2,1,0:T(8,128)(2,1)} %bitcast.20), channel_id=1, replica_groups=mesh['frame'=8,'tile'=16] {'frame','tile'}, dimensions={0} | all-to-all | bytes 3145728 | tf_op jit(solution)/shard_map/all_to_all | solution.py:298
  121.8 12.9 %time_backward.1 = bf16[8,2,32,768]{3,2,1,0:T(8,128)(2,1)} custom-call(bf16[8,2,32,768]{3,2,1,0:T(8,128)(2,1)} %bitcast.17, bf16[4,256,768]{2,1,0:T(8,128)(2,1)} %bitcast.18, bf16[256,768]{1,0:T(8,128)(2,1)} %get-tuple-element.8.hidden_ref, bf16[256,2304]{1,0:T(8,128)(2,1)} %get-tuple-element.9.qkv_ref, bf16[256,768]{1,0:T(8,128)(2,1)} %get-tuple-element.10.attended_ref, ...), custom_call_target="tpu_custom_call" | custom-call | tf_op jit(solution)/shard_map/time_backward/pallas_call | solution.py:302
  134.6 16.2 %all_to_all.22 = bf16[8,2,32,768]{3,2,1,0:T(8,128)(2,1)S(1)} all-to-all(bf16[8,2,32,768]{3,2,1,0:T(8,128)(2,1)} %time_backward.1), channel_id=1, replica_groups=mesh['frame'=8,'tile'=16] {'frame'}, dimensions={0} | all-to-all | bytes 1572864 | tf_op jit(solution)/shard_map/all_to_all | solution.py:312
  150.8 0.1 fusion
  150.9 0.9 copy_bitcast_fusion.1
Async XLA Ops:
  0.6 8.5 %copy-start.1 = (f32[768]{0:T(1024)S(1)}, f32[768]{0:T(1024)}, u32[]{:S(2)}) copy-start(f32[768]{0:T(1024)} %param.9) | copy-start | bytes 9220
  0.6 9.1 %copy-start.2 = (f32[768]{0:T(1024)S(1)}, f32[768]{0:T(1024)}, u32[]{:S(2)}) copy-start(f32[768]{0:T(1024)} %param.12) | copy-start | bytes 9220
  2.7 19.3 %all-to-all-start = ((bf16[8,2,4,8,768]{4,3,2,1,0:T(8,128)(2,1)}), bf16[8,2,4,8,768]{4,3,2,1,0:T(8,128)(2,1)S(1)}, u32[]{:S(2)}, u32[]{:S(2)}) async-start(bf16[8,2,4,8,768]{4,3,2,1,0:T(8,128)(2,1)} %copy_bitcast_fusion), calls=%async_computation | async-start | bytes 1572864 | tf_op jit(solution)/shard_map/all_to_all | solution.py:255
  22.0 0.9 copy-start

commit v2 on v1

--- a/solution.py
+++ b/solution.py
@@ -12,8 +12,8 @@
 F32 = jnp.float32
 BF16 = jnp.bfloat16
 VMEM = pl.BlockSpec(memory_space=pltpu.VMEM)
-ANY = pl.BlockSpec(memory_space=pl.ANY)
-LIMIT = 56 * 1024 * 1024
+HBM = pl.BlockSpec(memory_space=pltpu.HBM)
+LIMIT = 32 * 1024 * 1024
 
 
 def dot(a, b):
@@ -48,16 +48,15 @@
 
 def time_forward_kernel(
     patches, groups,
-    both_ref, gain_time_ref, gain_space_ref, qkv_time_hbm, out_time_hbm, qkv_space_hbm, out_space_hbm,
+    both_ref, gain_time_ref, gain_space_ref, qkv_time_hbm, out_time_ref, qkv_space_hbm, out_space_ref,
     send_ref, hidden_ref, qkv_ref, attended_ref, prob_ref,
-    qkv_time_ref, out_time_ref, qkv_space_ref, out_space_ref, sems,
+    qkv_time_ref, qkv_space_ref, sems,
 ):
     copies = [
         pltpu.make_async_copy(src, dst, sems.at[n])
-        for n, (src, dst) in enumerate((
-            (qkv_time_hbm, qkv_time_ref), (out_space_hbm, out_space_ref),
-            (out_time_hbm, out_time_ref), (qkv_space_hbm, qkv_space_ref),
-        ))
+        for n, (src, dst) in enumerate(
+            ((qkv_time_hbm, qkv_time_ref), (qkv_space_hbm, qkv_space_ref))
+        )
     ]
     for copy in copies:
         copy.start()
@@ -71,7 +70,6 @@
     copies[0].wait()
     qkv = dot(normed_half, qkv_time_ref[...]).astype(BF16)
     qkv_ref[...] = qkv
-    copies[1].wait()
     grad_out = dot_last(cotangent, out_space_ref[...]).astype(BF16)
     qkv_t = qkv.T
     mask = same_patch(tokens, patches)
@@ -87,12 +85,11 @@
         outputs.append(dot(values_t, prob))
     attended = jnp.concatenate(outputs, axis=0).T.astype(BF16)
     attended_ref[...] = attended
-    copies[2].wait()
     hidden = (tokens_in + dot(attended, out_time_ref[...])).astype(BF16)
     hidden_ref[...] = hidden
     normed_space, _ = norm_stats(hidden.astype(F32))
     space_half = (normed_space * gain_space_ref[...]).astype(BF16)
-    copies[3].wait()
+    copies[1].wait()
     space = dot(space_half, qkv_space_ref[...]).astype(BF16)
     for g in range(groups):
         send_ref[g] = jnp.concatenate(
@@ -102,7 +99,9 @@
         )
 
 
-def space_kernel(heads, block, got_ref, back_ref, nat, tra, out_t, grad_t, grad_key, grad_value):
+def space_kernel(
+    heads, block, together, got_ref, back_ref, nat, tra, out_t, grad_t, grad_key, grad_value
+):
     tokens, width = got_ref.shape
     part = width // 4
     size = part // heads
@@ -112,66 +111,58 @@
     for n in range(4):
         for h in range(heads):
             at = n * part + h * size
-            nat[n, h] = got[:, at : at + size]
+            if n in (1, 2):
+                nat[n - 1, h] = got[:, at : at + size]
             piece = got_t[at : at + size]
-            tra[n, h] = piece * jnp.asarray(scale, BF16) if n == 0 else piece
+            tra[n, h, :size] = piece * jnp.asarray(scale, BF16) if n == 0 else piece
+            if n == 2:
+                tra[n, h, size:] = jnp.ones((tra.shape[2] - size, tokens), BF16)
+    grad_key[...] = jnp.zeros_like(grad_key)
+    grad_value[...] = jnp.zeros_like(grad_value)
     blocks = tokens // block
 
+    def attention(t):
+        h = t // blocks
+        here = pl.ds(pl.multiple_of(t % blocks * block, block), block)
+        query_t = tra[0, h, :size, here]
+        grad_out_t = tra[3, h, :size, here]
+        scores = dot(nat[0, h], query_t)
+        yield
+        weights = jnp.exp(scores - jnp.max(scores, axis=0, keepdims=True)).astype(BF16)
+        yield
+        sums = dot(tra[2, h], weights)
+        inverse = 1.0 / sums[size : size + 1]
+        attended_t = (sums[:size] * inverse).astype(BF16)
+        out_t[h, :, here] = attended_t
+        delta = jnp.sum(grad_out_t.astype(F32) * attended_t.astype(F32), axis=0, keepdims=True)
+        grad_prob = dot(nat[1, h], grad_out_t)
+        grad_scores = (weights.astype(F32) * (grad_prob - delta)).astype(BF16)
+        yield
+        grad_t[h, :, here] = dot(tra[1, h, :size], grad_scores) * (inverse * scale)
+        grad_key[h] += dot_last(grad_scores, (query_t.astype(F32) * inverse).astype(BF16))
+        grad_value[h] += dot_last(weights, (grad_out_t.astype(F32) * inverse).astype(BF16))
+        yield
+
     def step(t, carry):
-        h = t // blocks
-        b = t % blocks
-        at = pl.multiple_of(b * block, block)
-        here = pl.ds(at, block)
-        scores = dot(nat[1, h], tra[0, h, :, here])
-        lifted = jnp.exp(scores - jnp.max(scores, axis=0, keepdims=True))
-        prob = lifted * (1.0 / jnp.sum(lifted, axis=0, keepdims=True))
-        prob_half = prob.astype(BF16)
-        attended_t = dot(tra[2, h], prob_half).astype(BF16)
-        out_t[h, :, here] = attended_t
-        grad_out_t = tra[3, h, :, here]
-        delta = jnp.sum(grad_out_t.astype(F32) * attended_t.astype(F32), axis=0, keepdims=True)
-        grad_prob = dot(nat[2, h], grad_out_t)
-        grad_scores = (prob * (grad_prob - delta)).astype(BF16)
-        grad_t[h, :, here] = dot(tra[1, h], grad_scores) * scale
-        key_terms = dot(grad_scores, nat[0, h, here, :])
-        value_terms = dot(prob_half, nat[3, h, here, :])
-
-        @pl.when(b == 0)
-        def _():
-            grad_key[h] = key_terms
-            grad_value[h] = value_terms
-
-        @pl.when(b > 0)
-        def _():
-            grad_key[h] += key_terms
-            grad_value[h] += value_terms
-
+        running = [attention(t * together + n) for n in range(together)]
+        for _ in range(4):
+            for one in running:
+                next(one)
         return carry
 
-    lax.fori_loop(0, heads * blocks, step, 0)
-    back_ref[:, :part * 2] = jnp.concatenate(
+    lax.fori_loop(0, heads * blocks // together, step, 0)
+    back_ref[:, : part * 2] = jnp.concatenate(
         [out_t[h].astype(F32) for h in range(heads)] + [grad_t[h] for h in range(heads)], axis=0
     ).T.astype(BF16)
-    back_ref[:, part * 2:] = jnp.concatenate(
-        [grad_key[h] * scale for h in range(heads)] + [grad_value[h] for h in range(heads)], axis=1
+    back_ref[:, part * 2 :] = jnp.concatenate(
+        [grad_key[h] for h in range(heads)] + [grad_value[h] for h in range(heads)], axis=1
     ).astype(BF16)
 
 
 def time_backward_kernel(
     both_ref, back_ref, hidden_ref, qkv_ref, attended_ref, prob_ref, gain_time_ref, gain_space_ref,
-    qkv_time_hbm, out_time_hbm, qkv_space_hbm, out_space_hbm,
-    out_ref,
-    qkv_time_ref, out_time_ref, qkv_space_ref, out_space_ref, sems,
+    qkv_time_ref, out_time_ref, qkv_space_ref, out_space_ref, out_ref,
 ):
-    copies = [
-        pltpu.make_async_copy(src, dst, sems.at[n])
-        for n, (src, dst) in enumerate((
-            (out_space_hbm, out_space_ref), (qkv_space_hbm, qkv_space_ref),
-            (out_time_hbm, out_time_ref), (qkv_time_hbm, qkv_time_ref),
-        ))
-    ]
-    for copy in copies:
-        copy.start()
     tokens, features = hidden_ref.shape
     groups = back_ref.shape[0]
     part = features // groups
@@ -185,18 +176,15 @@
         )
 
     hidden = hidden_ref[...].astype(F32)
-    copies[0].wait()
     block_output = (hidden + dot(column(0), out_space_ref[...])).astype(BF16)
     out_ref[:, 0] = block_output.reshape(shape)
     grad_qkv = jnp.concatenate([column(1), column(2), column(3)], axis=1)
-    copies[1].wait()
     grad_normed = dot_last(grad_qkv, qkv_space_ref[...])
     normed, inverse = norm_stats(hidden)
     cotangent = both_ref[:, 1].reshape(tokens, features).astype(F32)
     grad_hidden = (
         cotangent + norm_backward(grad_normed, gain_space_ref[...], normed, inverse)
     ).astype(BF16)
-    copies[2].wait()
     grad_out = dot_last(grad_hidden, out_time_ref[...]).astype(BF16)
     qkv = qkv_ref[...]
     keys_t = qkv[:, features : 2 * features].T
@@ -221,7 +209,6 @@
         ],
         axis=1,
     )
-    copies[3].wait()
     grad_normed_time = dot_last(grad_qkv_time, qkv_time_ref[...])
     tokens_in = both_ref[:, 0].reshape(tokens, features).astype(F32)
     normed_time, inverse_time = norm_stats(tokens_in)
@@ -244,8 +231,8 @@
     heads = HEADS // groups
     part = features // groups
     params = pltpu.CompilerParams(vmem_limit_bytes=LIMIT)
-    gain_time, gain_space = gain_time[None], gain_space[None]
     weights = (qkv_time, out_time, qkv_space, out_space)
+    far = lambda w: pltpu.with_memory_space_constraint(w, pltpu.HBM)
 
     def shaped(shape, dtype=BF16):
         return jax.ShapeDtypeStruct(shape, dtype)
@@ -255,7 +242,6 @@
     both = lax.all_to_all(both, "frame", 0, 0)
     both = both.reshape(frame_count, 2, frames * own_patches, features)
 
-    weight_scratch = [pltpu.VMEM(w.shape, w.dtype) for w in weights] + [pltpu.SemaphoreType.DMA((4,))]
     send, hidden, qkv, attended, prob = pl.pallas_call(
         functools.partial(time_forward_kernel, own_patches, groups),
         out_shape=(
@@ -265,12 +251,16 @@
             shaped((tokens, features)),
             shaped((HEADS, tokens, tokens)),
         ),
-        in_specs=[VMEM] * 3 + [ANY] * 4,
+        in_specs=[VMEM] * 3 + [HBM, VMEM, HBM, VMEM],
         out_specs=[VMEM] * 5,
-        scratch_shapes=weight_scratch,
+        scratch_shapes=[
+            pltpu.VMEM(qkv_time.shape, BF16),
+            pltpu.VMEM(qkv_space.shape, BF16),
+            pltpu.SemaphoreType.DMA((2,)),
+        ],
         compiler_params=params,
         name="time_forward",
-    )(both, gain_time, gain_space, *weights)
+    )(both, gain_time, gain_space, far(qkv_time), out_time, far(qkv_space), out_space)
 
     got = lax.all_to_all(
         send.reshape(devices, own_patches, 4 * part), ("frame", "tile"), 0, 0
@@ -279,13 +269,13 @@
     rows = devices * own_patches
     size = features // HEADS
     back = pl.pallas_call(
-        functools.partial(space_kernel, heads, 256),
+        functools.partial(space_kernel, heads, 256, 4),
         out_shape=shaped((rows, 4 * part)),
         in_specs=[VMEM],
         out_specs=VMEM,
         scratch_shapes=[
-            pltpu.VMEM((4, heads, rows, size), BF16),
-            pltpu.VMEM((4, heads, size, rows), BF16),
+            pltpu.VMEM((2, heads, rows, size), BF16),
+            pltpu.VMEM((4, heads, size + 16, rows), BF16),
             pltpu.VMEM((heads, size, rows), BF16),
             pltpu.VMEM((heads, size, rows), F32),
             pltpu.VMEM((heads, rows, size), F32),
@@ -302,9 +292,8 @@
     result = pl.pallas_call(
         time_backward_kernel,
         out_shape=shaped(both.shape),
-        in_specs=[VMEM] * 8 + [ANY] * 4,
+        in_specs=[VMEM] * 12,
         out_specs=VMEM,
-        scratch_shapes=weight_scratch,
         compiler_params=params,
         name="time_backward",
     )(both, back, hidden, qkv, attended, prob, gain_time, gain_space, *weights)

time: 152 us -> 127 us (0.84)
  Pallas kernels: 49.5 us -> 28.1 us
  blocking collectives: 78.3 us -> 95.3 us
  waiting for transfers between devices: 11.7 us -> 0 us
  starting transfers between devices: 6.41 us -> 0 us
  local copies, waits for them, and re-layouts: 3.07 us -> 1.01 us
    all_to_all x0 -> x1, blocking collectives: none -> 19.2 us  [local(): both = lax.all_to_all(both, 'frame', 0, 0)]
    pallas_call x1, Pallas kernels: 24.9 us -> 11.9 us  [local(): pl.pallas_call(functools.partial(space_kernel, heads, 256, 4), out_shape=...]
    all_to_all x1 -> x0, waiting for transfers between devices: 11.7 us -> none  [local(): both = lax.all_to_all(both, 'frame', 0, 0)]
    all_to_all x1 -> x0, starting transfers between devices: 6.41 us -> none  [local(): both = lax.all_to_all(both, 'frame', 0, 0)]
    pallas_call x1, Pallas kernels: 12.9 us -> 7.09 us  [local(): pl.pallas_call(time_backward_kernel, out_shape=shaped(both.shape), in_spe...]
    pallas_call x1, Pallas kernels: 11.8 us -> 9.14 us  [local(): pl.pallas_call(functools.partial(time_forward_kernel, own_patches, groups...]
  transfers between devices with their start and end apart: 1 -> 0, of which waited for: 1 -> 0; matrix products, arithmetic and copies ran while one was open for 1% -> 0% of each run, Pallas kernels for 0% -> 0%
where the time goes in v2:
time: 127 us; the launch traced here: 126 us
  blocking collectives  95.3 us (75%)
  Pallas kernels  28.1 us (22%)
  other arithmetic  1.34 us (1%)
    all_to_all x1, blocking collectives, local(): lax.all_to_all(send.reshape(devices, own_patches, 4 * part), ('frame', 't...  32.1 us
    all_to_all x1, blocking collectives, local(): lax.all_to_all(back.reshape(devices, own_patches, 4 * part), ('frame', 't...  28.8 us
    all_to_all x1, blocking collectives, local(): both = lax.all_to_all(both, 'frame', 0, 0)  19.2 us
    all_to_all x1, blocking collectives, local(): result = lax.all_to_all(result, 'frame', 0, 0)  15.2 us
    pallas_call x1, Pallas kernels, local(): pl.pallas_call(functools.partial(space_kernel, heads, 256, 4), out_shape=...  11.9 us
    pallas_call x1, Pallas kernels, local(): pl.pallas_call(functools.partial(time_forward_kernel, own_patches, groups...  9.14 us
    pallas_call x1, Pallas kernels, local(): pl.pallas_call(time_backward_kernel, out_shape=shaped(both.shape), in_spe...  7.09 us

profile of v2, /device:TPU:0, one launch (start us, length us, event | category | flops | bytes accessed | tf_op | source)
XLA Modules:
  0.0 126.5 jit_solution(16996765391706998443)
XLA Ops:
  0.6 0.0 copy-start.2
  0.6 0.0 copy-start.3
  0.7 0.0 copy-start.4
  0.7 0.0 copy-start.5
  0.7 1.3 %copy_bitcast_fusion = bf16[8,2,4,8,768]{4,3,2,1,0:T(8,128)(2,1)S(1)} fusion(bf16[1,4,8,8,768]{4,3,2,1,0:T(8,128)(2,1)} %bitcast.23, bf16[1,4,8,8,768]{4,3,2,1,0:T(8,128)(2,1)} %bitcast.24), kind=kLoop, calls=%fused_computation.1 | loop fusion | flops 393216 | bytes 1572864 | tf_op jit(solution)/shard_map/transpose | solution.py:241
  2.0 19.2 %all_to_all.20 = bf16[8,2,4,8,768]{4,3,2,1,0:T(8,128)(2,1)S(1)} all-to-all(bf16[8,2,4,8,768]{4,3,2,1,0:T(8,128)(2,1)S(1)} %copy_bitcast_fusion), channel_id=1, replica_groups=mesh['frame'=8,'tile'=16] {'frame'}, dimensions={0} | all-to-all | bytes 1572864 | tf_op jit(solution)/shard_map/all_to_all | solution.py:242
  21.2 0.0 copy-done.2
  21.2 0.0 copy-done.3
  21.2 0.0 copy-done.4
  21.2 0.0 copy-done.5
  21.2 9.1 %time_forward.1 = (bf16[4,256,768]{2,1,0:T(8,128)(2,1)S(1)}, bf16[256,768]{1,0:T(8,128)(2,1)S(1)}, bf16[256,2304]{1,0:T(8,128)(2,1)S(1)}, bf16[256,768]{1,0:T(8,128)(2,1)S(1)}, bf16[12,256,256]{2,1,0:T(8,128)(2,1)S(1)}) custom-call(bf16[8,2,32,768]{3,2,1,0:T(8,128)(2,1)S(1)} %bitcast.16, f32[768]{0:T(1024)S(1)} %copy-done.4, f32[768]{0:T(1024)S(1)} %copy-done.5, ...), custom_call_target="tpu_custom_call" | custom-call | tf_op jit(solution)/shard_map/time_forward/pallas_call | solution.py:245
  30.4 0.0 copy-start.1
  30.4 32.1 %all_to_all.21 = bf16[128,8,768]{2,1,0:T(8,128)(2,1)S(1)} all-to-all(bf16[128,8,768]{2,1,0:T(8,128)(2,1)S(1)} %bitcast.21), channel_id=1, replica_groups=mesh['frame'=8,'tile'=16] {'frame','tile'}, dimensions={0} | all-to-all | bytes 3145728 | tf_op jit(solution)/shard_map/all_to_all | solution.py:265
  62.5 0.0 copy-start
  62.5 11.9 %space_attention.1 = bf16[1024,768]{1,0:T(8,128)(2,1)S(1)} custom-call(bf16[1024,768]{1,0:T(8,128)(2,1)S(1)} %bitcast.19), custom_call_target="tpu_custom_call" | custom-call | tf_op jit(solution)/shard_map/space_attention/pallas_call | solution.py:271
  74.3 28.8 %all_to_all.22 = bf16[128,8,768]{2,1,0:T(8,128)(2,1)S(1)} all-to-all(bf16[128,8,768]{2,1,0:T(8,128)(2,1)S(1)} %bitcast.20), channel_id=1, replica_groups=mesh['frame'=8,'tile'=16] {'frame','tile'}, dimensions={0} | all-to-all | bytes 3145728 | tf_op jit(solution)/shard_map/all_to_all | solution.py:288
  103.2 0.0 copy-done.1
  103.2 0.0 copy-done
  103.2 7.1 %time_backward.1 = bf16[8,2,32,768]{3,2,1,0:T(8,128)(2,1)S(1)} custom-call(bf16[8,2,32,768]{3,2,1,0:T(8,128)(2,1)S(1)} %bitcast.17, bf16[4,256,768]{2,1,0:T(8,128)(2,1)S(1)} %bitcast.18, bf16[256,768]{1,0:T(8,128)(2,1)S(1)} %get-tuple-element.8.hidden_ref, bf16[256,2304]{1,0:T(8,128)(2,1)S(1)} %get-tuple-element.9.qkv_ref, ...), custom_call_target="tpu_custom_call" | custom-call | tf_op jit(solution)/shard_map/time_backward/pallas_call | solution.py:292
  110.3 15.2 %all_to_all.23 = bf16[8,2,32,768]{3,2,1,0:T(8,128)(2,1)S(1)} all-to-all(bf16[8,2,32,768]{3,2,1,0:T(8,128)(2,1)S(1)} %time_backward.1), channel_id=1, replica_groups=mesh['frame'=8,'tile'=16] {'frame'}, dimensions={0} | all-to-all | bytes 1572864 | tf_op jit(solution)/shard_map/all_to_all | solution.py:301
  125.5 0.1 fusion
  125.6 0.9 copy_bitcast_fusion.1
Async XLA Ops:
  0.6 20.6 %copy-start.2 = (bf16[768,768]{1,0:T(8,128)(2,1)S(1)}, bf16[768,768]{1,0:T(8,128)(2,1)}, u32[]{:S(2)}) copy-start(bf16[768,768]{1,0:T(8,128)(2,1)} %out_time_ref.3) | copy-start | bytes 3538948
  0.6 20.6 %copy-start.3 = (bf16[768,768]{1,0:T(8,128)(2,1)S(1)}, bf16[768,768]{1,0:T(8,128)(2,1)}, u32[]{:S(2)}) copy-start(bf16[768,768]{1,0:T(8,128)(2,1)} %out_space_ref.3) | copy-start | bytes 3538948
  0.7 20.6 %copy-start.4 = (f32[768]{0:T(1024)S(1)}, f32[768]{0:T(1024)}, u32[]{:S(2)}) copy-start(f32[768]{0:T(1024)} %gain_time_ref.3) | copy-start | bytes 9220
  0.7 20.6 %copy-start.5 = (f32[768]{0:T(1024)S(1)}, f32[768]{0:T(1024)}, u32[]{:S(2)}) copy-start(f32[768]{0:T(1024)} %gain_space_ref.3) | copy-start | bytes 9220
  30.4 72.8 %copy-start.1 = (bf16[768,2304]{1,0:T(8,128)(2,1)S(1)}, bf16[768,2304]{1,0:T(8,128)(2,1)}, u32[]{:S(2)}) copy-start(bf16[768,2304]{1,0:T(8,128)(2,1)} %qkv_space_ref.1) | copy-start | bytes 10616836
  62.5 40.7 %copy-start = (bf16[768,2304]{1,0:T(8,128)(2,1)S(1)}, bf16[768,2304]{1,0:T(8,128)(2,1)}, u32[]{:S(2)}) copy-start(bf16[768,2304]{1,0:T(8,128)(2,1)} %qkv_time_ref.1) | copy-start | bytes 10616836

commit v3 on v2

--- a/solution.py
+++ b/solution.py
@@ -40,23 +40,46 @@
     )
 
 
-def same_patch(tokens, patches):
-    rows = lax.broadcasted_iota(jnp.int32, (tokens, tokens), 0)
-    columns = lax.broadcasted_iota(jnp.int32, (tokens, tokens), 1)
-    return (rows % patches) == (columns % patches)
+def in_turn(running):
+    running, ended = list(running), {}
+    while len(ended) < len(running):
+        for n, one in enumerate(running):
+            if n not in ended:
+                try:
+                    next(one)
+                except StopIteration as stop:
+                    ended[n] = stop.value
+    return [ended[n] for n in range(len(running))]
+
+
+def fetch_kernel(qkv_hbm, query_ref, key_ref, sems):
+    depth = qkv_hbm.shape[0]
+    copies = [
+        pltpu.make_async_copy(qkv_hbm.at[:, pl.ds(n * depth, depth)], ref, sems.at[n])
+        for n, ref in enumerate((query_ref, key_ref))
+    ]
+    for copy in copies:
+        copy.start()
+    for copy in copies:
+        copy.wait()
 
 
 def time_forward_kernel(
-    patches, groups,
-    both_ref, gain_time_ref, gain_space_ref, qkv_time_hbm, out_time_ref, qkv_space_hbm, out_space_ref,
-    send_ref, hidden_ref, qkv_ref, attended_ref, prob_ref,
-    qkv_time_ref, qkv_space_ref, sems,
+    patches, groups, together,
+    both_ref, gain_time_ref, gain_space_ref, query_time_ref, key_time_ref,
+    qkv_time_hbm, out_time_hbm, qkv_space_hbm, out_space_hbm,
+    send_ref, hidden_ref, qkv_ref, attended_ref, weights_ref, inverse_ref,
+    value_time_ref, out_space_ref, out_time_ref, qkv_space_ref, sems,
 ):
+    depth = qkv_time_hbm.shape[0]
     copies = [
         pltpu.make_async_copy(src, dst, sems.at[n])
-        for n, (src, dst) in enumerate(
-            ((qkv_time_hbm, qkv_time_ref), (qkv_space_hbm, qkv_space_ref))
-        )
+        for n, (src, dst) in enumerate((
+            (qkv_time_hbm.at[:, pl.ds(2 * depth, depth)], value_time_ref),
+            (out_space_hbm, out_space_ref),
+            (out_time_hbm, out_time_ref),
+            (qkv_space_hbm, qkv_space_ref),
+        ))
     ]
     for copy in copies:
         copy.start()
@@ -67,29 +90,45 @@
     cotangent = both_ref[:, 1].reshape(tokens, features)
     normed, _ = norm_stats(tokens_in)
     normed_half = (normed * gain_time_ref[...]).astype(BF16)
+    queries = dot(normed_half, query_time_ref[...]).astype(BF16)
+    keys = dot(normed_half, key_time_ref[...]).astype(BF16)
     copies[0].wait()
-    qkv = dot(normed_half, qkv_time_ref[...]).astype(BF16)
+    values = dot(normed_half, value_time_ref[...]).astype(BF16)
+    qkv = jnp.concatenate([queries, keys, values], axis=1)
     qkv_ref[...] = qkv
+    copies[1].wait()
     grad_out = dot_last(cotangent, out_space_ref[...]).astype(BF16)
     qkv_t = qkv.T
-    mask = same_patch(tokens, patches)
+    queries_t = qkv_t[:features] * jnp.asarray(size ** -0.5, BF16)
+    rows = lax.broadcasted_iota(jnp.int32, (tokens, tokens), 0)
+    columns = lax.broadcasted_iota(jnp.int32, (tokens, tokens), 1)
+    bias = jnp.where((rows % patches) == (columns % patches), 0.0, -1e30)
+    ones = jnp.ones((16, tokens), BF16)
+
+    def attention(h):
+        keys = qkv[:, features + h * size : features + (h + 1) * size]
+        scores = dot(keys, queries_t[h * size : (h + 1) * size]) + bias
+        yield
+        weights = jnp.exp(scores - jnp.max(scores, axis=0, keepdims=True)).astype(BF16)
+        weights_ref[h] = weights
+        yield
+        values_t = qkv_t[2 * features + h * size : 2 * features + (h + 1) * size]
+        sums = dot(jnp.concatenate([values_t, ones], axis=0), weights)
+        inverse = 1.0 / sums[size : size + 1]
+        inverse_ref[h : h + 1] = inverse
+        return sums[:size] * inverse
+
     outputs = []
-    for h in range(HEADS):
-        keys = qkv[:, features + h * size : features + (h + 1) * size]
-        queries_t = qkv_t[h * size : (h + 1) * size] * jnp.asarray(size ** -0.5, BF16)
-        scores = jnp.where(mask, dot(keys, queries_t), -1e30)
-        lifted = jnp.exp(scores - jnp.max(scores, axis=0, keepdims=True))
-        prob = (lifted / jnp.sum(lifted, axis=0, keepdims=True)).astype(BF16)
-        prob_ref[h] = prob
-        values_t = qkv_t[2 * features + h * size : 2 * features + (h + 1) * size]
-        outputs.append(dot(values_t, prob))
+    for h in range(0, HEADS, together):
+        outputs += in_turn(attention(h + n) for n in range(together))
     attended = jnp.concatenate(outputs, axis=0).T.astype(BF16)
     attended_ref[...] = attended
+    copies[2].wait()
     hidden = (tokens_in + dot(attended, out_time_ref[...])).astype(BF16)
     hidden_ref[...] = hidden
     normed_space, _ = norm_stats(hidden.astype(F32))
     space_half = (normed_space * gain_space_ref[...]).astype(BF16)
-    copies[1].wait()
+    copies[3].wait()
     space = dot(space_half, qkv_space_ref[...]).astype(BF16)
     for g in range(groups):
         send_ref[g] = jnp.concatenate(
@@ -141,13 +180,9 @@
         grad_t[h, :, here] = dot(tra[1, h, :size], grad_scores) * (inverse * scale)
         grad_key[h] += dot_last(grad_scores, (query_t.astype(F32) * inverse).astype(BF16))
         grad_value[h] += dot_last(weights, (grad_out_t.astype(F32) * inverse).astype(BF16))
-        yield
 
     def step(t, carry):
-        running = [attention(t * together + n) for n in range(together)]
-        for _ in range(4):
-            for one in running:
-                next(one)
+        in_turn(attention(t * together + n) for n in range(together))
         return carry
 
     lax.fori_loop(0, heads * blocks // together, step, 0)
@@ -160,7 +195,8 @@
 
 
 def time_backward_kernel(
-    both_ref, back_ref, hidden_ref, qkv_ref, attended_ref, prob_ref, gain_time_ref, gain_space_ref,
+    together,
+    both_ref, back_ref, hidden_ref, qkv_ref, attended_ref, weights_ref, inverse_ref, gain_time_ref, gain_space_ref,
     qkv_time_ref, out_time_ref, qkv_space_ref, out_space_ref, out_ref,
 ):
     tokens, features = hidden_ref.shape
@@ -190,17 +226,27 @@
     keys_t = qkv[:, features : 2 * features].T
     grad_out_t = grad_out.T
     product_t = (grad_out.astype(F32) * attended_ref[...].astype(F32)).T
-    queries_grad, keys_grad, values_grad = [], [], []
-    for h in range(HEADS):
+    queries_t = qkv[:, :features].T
+
+    def attention(h):
         own = slice(h * size, (h + 1) * size)
         delta = jnp.sum(product_t[own], axis=0, keepdims=True)
-        prob = prob_ref[h]
+        weights = weights_ref[h]
+        inverse = inverse_ref[h : h + 1]
         values = qkv[:, 2 * features + h * size : 2 * features + (h + 1) * size]
         grad_prob = dot(values, grad_out_t[own])
-        grad_scores = (prob.astype(F32) * (grad_prob - delta)).astype(BF16)
-        queries_grad.append(dot(keys_t[own], grad_scores) * scale)
-        keys_grad.append(dot(grad_scores, qkv[:, own]) * scale)
-        values_grad.append(dot(prob, grad_out[:, own]))
+        yield
+        grad_scores = (weights.astype(F32) * (grad_prob - delta)).astype(BF16)
+        yield
+        queries_grad = dot(keys_t[own], grad_scores) * (inverse * scale)
+        keys_grad = dot_last(grad_scores, (queries_t[own].astype(F32) * inverse).astype(BF16))
+        values_grad = dot_last(weights, (grad_out_t[own].astype(F32) * inverse).astype(BF16))
+        return queries_grad, keys_grad * scale, values_grad
+
+    ended = []
+    for h in range(0, HEADS, together):
+        ended += in_turn(attention(h + n) for n in range(together))
+    queries_grad, keys_grad, values_grad = zip(*ended)
     grad_qkv_time = jnp.concatenate(
         [
             jnp.concatenate(queries_grad, axis=0).T.astype(BF16),
@@ -231,36 +277,49 @@
     heads = HEADS // groups
     part = features // groups
     params = pltpu.CompilerParams(vmem_limit_bytes=LIMIT)
-    weights = (qkv_time, out_time, qkv_space, out_space)
-    far = lambda w: pltpu.with_memory_space_constraint(w, pltpu.HBM)
-
     def shaped(shape, dtype=BF16):
         return jax.ShapeDtypeStruct(shape, dtype)
+
+    weights = (qkv_time, out_time, qkv_space, out_space)
+    far = [pltpu.with_memory_space_constraint(w, pltpu.HBM) for w in weights]
+    near = pl.pallas_call(
+        fetch_kernel,
+        out_shape=(shaped((features, features)),) * 2,
+        in_specs=[HBM],
+        out_specs=[VMEM] * 2,
+        scratch_shapes=[pltpu.SemaphoreType.DMA((2,))],
+        compiler_params=pltpu.CompilerParams(vmem_limit_bytes=8 * 1024 * 1024),
+        cost_estimate=pl.CostEstimate(flops=0, bytes_accessed=20 * 1024 * 1024, transcendentals=0),
+        name="fetch_weights",
+    )(far[0])
 
     both = jnp.stack([patch_tokens, cotangent])
     both = both.reshape(2, frames, frame_count, own_patches, features).transpose(2, 0, 1, 3, 4)
     both = lax.all_to_all(both, "frame", 0, 0)
     both = both.reshape(frame_count, 2, frames * own_patches, features)
 
-    send, hidden, qkv, attended, prob = pl.pallas_call(
-        functools.partial(time_forward_kernel, own_patches, groups),
+    send, hidden, qkv, attended, scores, inverse = pl.pallas_call(
+        functools.partial(time_forward_kernel, own_patches, groups, 6),
         out_shape=(
             shaped((groups, tokens, 4 * part)),
             shaped((tokens, features)),
             shaped((tokens, 3 * features)),
             shaped((tokens, features)),
             shaped((HEADS, tokens, tokens)),
+            shaped((HEADS, tokens), F32),
         ),
-        in_specs=[VMEM] * 3 + [HBM, VMEM, HBM, VMEM],
-        out_specs=[VMEM] * 5,
+        in_specs=[VMEM] * 5 + [HBM] * 4,
+        out_specs=[VMEM] * 6,
         scratch_shapes=[
-            pltpu.VMEM(qkv_time.shape, BF16),
+            pltpu.VMEM((features, features), BF16),
+            pltpu.VMEM((features, features), BF16),
+            pltpu.VMEM((features, features), BF16),
             pltpu.VMEM(qkv_space.shape, BF16),
-            pltpu.SemaphoreType.DMA((2,)),
+            pltpu.SemaphoreType.DMA((4,)),
         ],
         compiler_params=params,
         name="time_forward",
-    )(both, gain_time, gain_space, far(qkv_time), out_time, far(qkv_space), out_space)
+    )(both, gain_time, gain_space, *near, *far)
 
     got = lax.all_to_all(
         send.reshape(devices, own_patches, 4 * part), ("frame", "tile"), 0, 0
@@ -269,7 +328,7 @@
     rows = devices * own_patches
     size = features // HEADS
     back = pl.pallas_call(
-        functools.partial(space_kernel, heads, 256, 4),
+        functools.partial(space_kernel, heads, 256, 12),
         out_shape=shaped((rows, 4 * part)),
         in_specs=[VMEM],
         out_specs=VMEM,
@@ -290,13 +349,13 @@
     ).reshape(groups, tokens, 4 * part)
 
     result = pl.pallas_call(
-        time_backward_kernel,
+        functools.partial(time_backward_kernel, 6),
         out_shape=shaped(both.shape),
-        in_specs=[VMEM] * 12,
+        in_specs=[VMEM] * 13,
         out_specs=VMEM,
         compiler_params=params,
         name="time_backward",
-    )(both, back, hidden, qkv, attended, prob, gain_time, gain_space, *weights)
+    )(both, back, hidden, qkv, attended, scores, inverse, gain_time, gain_space, *weights)
 
     result = lax.all_to_all(result, "frame", 0, 0)
     result = result.reshape(frame_count, 2, frames, own_patches, features).transpose(1, 2, 0, 3, 4)

time: 127 us -> 122 us (0.961)
  blocking collectives: 95.3 us -> 75.9 us
  waiting for transfers between devices: 0 us -> 11.2 us
  starting transfers between devices: 0 us -> 6.41 us
  Pallas kernels: 28.1 us -> 24.2 us
    all_to_all x1 -> x0, blocking collectives: 19.2 us -> none  [local(): both = lax.all_to_all(both, 'frame', 0, 0)]
    all_to_all x0 -> x1, waiting for transfers between devices: none -> 11.2 us  [local(): both = lax.all_to_all(both, 'frame', 0, 0)]
    all_to_all x0 -> x1, starting transfers between devices: none -> 6.41 us  [local(): both = lax.all_to_all(both, 'frame', 0, 0)]
    pallas_call x1, Pallas kernels: 9.14 us -> 5.7 us  [local(): pl.pallas_call(functools.partial(time_forward_kernel, own_patches, groups...]
    pallas_call x2 -> x3, Pallas kernels: 18.9 us -> 18.5 us  [the longest x1 10.9 us: local(): pl.pallas_call(functools.partial(space_kernel, heads, 256, 12), out_shape...]
  transfers between devices with their start and end apart: 0 -> 1, of which waited for: 0 -> 1; matrix products, arithmetic and copies ran while one was open for 0% -> 0% of each run, Pallas kernels for 0% -> 1%
where the time goes in v3:
time: 122 us; the launch traced here: 121 us
  blocking collectives  75.9 us (62%)
  Pallas kernels  24.2 us (20%)
  waiting for transfers between devices  11.2 us (9%)
  starting transfers between devices  6.41 us (5%)
  other arithmetic  2.09 us (2%)
    all_to_all x1, blocking collectives, local(): lax.all_to_all(send.reshape(devices, own_patches, 4 * part), ('frame', 't...  31.8 us
    all_to_all x1, blocking collectives, local(): lax.all_to_all(back.reshape(devices, own_patches, 4 * part), ('frame', 't...  28.8 us
    all_to_all x1, blocking collectives, local(): result = lax.all_to_all(result, 'frame', 0, 0)  15.2 us
    all_to_all x1, waiting for transfers between devices, local(): both = lax.all_to_all(both, 'frame', 0, 0)  11.2 us
    pallas_call x1, Pallas kernels, local(): pl.pallas_call(functools.partial(space_kernel, heads, 256, 12), out_shape...  10.9 us
    all_to_all x1, starting transfers between devices, local(): both = lax.all_to_all(both, 'frame', 0, 0)  6.41 us
    pallas_call x1, Pallas kernels, local(): pl.pallas_call(functools.partial(time_backward_kernel, 6), out_shape=shap...  5.85 us
    pallas_call x1, Pallas kernels, local(): pl.pallas_call(functools.partial(time_forward_kernel, own_patches, groups...  5.7 us
  transfers between devices with their start and end apart: 1, of which 1 were waited for; matrix products, arithmetic and copies ran while one was open for 0% of the time, Pallas kernels for 1%

profile of v3, /device:TPU:0, one launch (start us, length us, event | category | flops | bytes accessed | tf_op | source)
XLA Modules:
  0.0 121.5 jit_solution(17335046027247575455)
XLA Ops:
  0.6 2.1 %copy_bitcast_fusion = bf16[8,2,4,8,768]{4,3,2,1,0:T(8,128)(2,1)} fusion(bf16[1,4,8,8,768]{4,3,2,1,0:T(8,128)(2,1)} %bitcast.23, bf16[1,4,8,8,768]{4,3,2,1,0:T(8,128)(2,1)} %bitcast.24), kind=kLoop, calls=%fused_computation.1 | loop fusion | flops 393216 | bytes 1572864 | tf_op jit(solution)/shard_map/transpose | solution.py:297
  2.7 6.4 %all-to-all-start = ((bf16[8,2,4,8,768]{4,3,2,1,0:T(8,128)(2,1)}), bf16[8,2,4,8,768]{4,3,2,1,0:T(8,128)(2,1)S(1)}, u32[]{:S(2)}, u32[]{:S(2)}) async-start(bf16[8,2,4,8,768]{4,3,2,1,0:T(8,128)(2,1)} %copy_bitcast_fusion), calls=%async_computation | async-start | bytes 1572864 | tf_op jit(solution)/shard_map/all_to_all | solution.py:298
  9.1 0.0 copy-start.4
  9.1 0.0 copy-start.5
  9.1 1.7 %fetch_weights.1 = (bf16[768,768]{1,0:T(8,128)(2,1)S(1)}, bf16[768,768]{1,0:T(8,128)(2,1)S(1)}) custom-call(bf16[768,2304]{1,0:T(8,128)(2,1)} %qkv_time_ref.1), custom_call_target="tpu_custom_call" | custom-call | bytes 20971520 | tf_op jit(solution)/shard_map/fetch_weights/pallas_call | solution.py:285
  10.8 11.2 %all-to-all-done = bf16[8,2,4,8,768]{4,3,2,1,0:T(8,128)(2,1)S(1)} async-done(((bf16[8,2,4,8,768]{4,3,2,1,0:T(8,128)(2,1)}), bf16[8,2,4,8,768]{4,3,2,1,0:T(8,128)(2,1)S(1)}, u32[]{:S(2)}, u32[]{:S(2)}) %all-to-all-start) | async-done | bytes 786464 | tf_op jit(solution)/shard_map/all_to_all | solution.py:298
  22.0 0.0 copy-done.4
  22.0 0.0 copy-done.5
  22.0 5.7 %time_forward.1 = (bf16[4,256,768]{2,1,0:T(8,128)(2,1)S(1)}, bf16[256,768]{1,0:T(8,128)(2,1)S(1)}, bf16[256,2304]{1,0:T(8,128)(2,1)S(1)}, bf16[256,768]{1,0:T(8,...) custom-call(bf16[8,2,32,768]{3,2,1,0:T(8,128)(2,1)S(1)} %bitcast.16, f32[768]{0:T(1024)S(1)} %copy-done.4, ...), custom_call_target="tpu_custom_call" | custom-call | tf_op jit(solution)/shard_map/time_forward/pallas_call | solution.py:301
  27.7 0.0 copy-start.1
  27.7 31.8 %all_to_all.20 = bf16[128,8,768]{2,1,0:T(8,128)(2,1)S(1)} all-to-all(bf16[128,8,768]{2,1,0:T(8,128)(2,1)S(1)} %bitcast.21), channel_id=1, replica_groups=mesh['frame'=8,'tile'=16] {'frame','tile'}, dimensions={0} | all-to-all | bytes 3145728 | tf_op jit(solution)/shard_map/all_to_all | solution.py:324
  59.6 0.0 copy-start
  59.6 10.9 %space_attention.1 = bf16[1024,768]{1,0:T(8,128)(2,1)S(1)} custom-call(bf16[1024,768]{1,0:T(8,128)(2,1)S(1)} %bitcast.19), custom_call_target="tpu_custom_call" | custom-call | tf_op jit(solution)/shard_map/space_attention/pallas_call | solution.py:330
  70.5 0.0 copy-start.2
  70.5 0.0 copy-start.3
  70.5 28.8 %all_to_all.21 = bf16[128,8,768]{2,1,0:T(8,128)(2,1)S(1)} all-to-all(bf16[128,8,768]{2,1,0:T(8,128)(2,1)S(1)} %bitcast.20), channel_id=1, replica_groups=mesh['frame'=8,'tile'=16] {'frame','tile'}, dimensions={0} | all-to-all | bytes 3145728 | tf_op jit(solution)/shard_map/all_to_all | solution.py:347
  99.4 0.0 copy-done.1
  99.4 0.0 copy-done
  99.4 0.0 copy-done.2
  99.4 0.0 copy-done.3
  99.4 5.9 %time_backward.1 = bf16[8,2,32,768]{3,2,1,0:T(8,128)(2,1)S(1)} custom-call(bf16[8,2,32,768]{3,2,1,0:T(8,128)(2,1)S(1)} %bitcast.17, bf16[4,256,768]{2,1,0:T(8,128)(2,1)S(1)} %bitcast.18, bf16[256,768]{1,0:T(8,128)(2,1)S(1)} %get-tuple-element.13.hidden_ref, bf16[256,2304]{1,0:T(8,128)(2,1)S(1)} %get-tuple-element.14.qkv_ref, ...), custom_call_target="tpu_custom_call" | custom-call | tf_op jit(solution)/shard_map/time_backward/pallas_call | solution.py:351
  105.3 15.2 %all_to_all.22 = bf16[8,2,32,768]{3,2,1,0:T(8,128)(2,1)S(1)} all-to-all(bf16[8,2,32,768]{3,2,1,0:T(8,128)(2,1)S(1)} %time_backward.1), channel_id=1, replica_groups=mesh['frame'=8,'tile'=16] {'frame'}, dimensions={0} | all-to-all | bytes 1572864 | tf_op jit(solution)/shard_map/all_to_all | solution.py:360
  120.5 0.1 fusion
  120.5 0.9 copy_bitcast_fusion.1
Async XLA Ops:
  2.7 19.3 %all-to-all-start = ((bf16[8,2,4,8,768]{4,3,2,1,0:T(8,128)(2,1)}), bf16[8,2,4,8,768]{4,3,2,1,0:T(8,128)(2,1)S(1)}, u32[]{:S(2)}, u32[]{:S(2)}) async-start(bf16[8,2,4,8,768]{4,3,2,1,0:T(8,128)(2,1)} %copy_bitcast_fusion), calls=%async_computation | async-start | bytes 1572864 | tf_op jit(solution)/shard_map/all_to_all | solution.py:298
  9.1 12.9 %copy-start.4 = (f32[768]{0:T(1024)S(1)}, f32[768]{0:T(1024)}, u32[]{:S(2)}) copy-start(f32[768]{0:T(1024)} %gain_time_ref.3) | copy-start | bytes 9220
  9.1 12.9 %copy-start.5 = (f32[768]{0:T(1024)S(1)}, f32[768]{0:T(1024)}, u32[]{:S(2)}) copy-start(f32[768]{0:T(1024)} %gain_space_ref.3) | copy-start | bytes 9220
  27.7 71.6 %copy-start.1 = (bf16[768,2304]{1,0:T(8,128)(2,1)S(1)}, bf16[768,2304]{1,0:T(8,128)(2,1)}, u32[]{:S(2)}) copy-start(bf16[768,2304]{1,0:T(8,128)(2,1)} %qkv_space_ref.1) | copy-start | bytes 10616836
  59.6 39.8 %copy-start = (bf16[768,2304]{1,0:T(8,128)(2,1)S(1)}, bf16[768,2304]{1,0:T(8,128)(2,1)}, u32[]{:S(2)}) copy-start(bf16[768,2304]{1,0:T(8,128)(2,1)} %qkv_time_ref.1) | copy-start | bytes 10616836
  70.5 28.9 %copy-start.2 = (bf16[768,768]{1,0:T(8,128)(2,1)S(1)}, bf16[768,768]{1,0:T(8,128)(2,1)}, u32[]{:S(2)}) copy-start(bf16[768,768]{1,0:T(8,128)(2,1)} %out_time_ref.1) | copy-start | bytes 3538948
  70.5 28.9 %copy-start.3 = (bf16[768,768]{1,0:T(8,128)(2,1)S(1)}, bf16[768,768]{1,0:T(8,128)(2,1)}, u32[]{:S(2)}) copy-start(bf16[768,768]{1,0:T(8,128)(2,1)} %out_space_ref.1) | copy-start | bytes 3538948

commit v4 on v3

--- a/solution.py
+++ b/solution.py
@@ -92,36 +92,39 @@
     normed_half = (normed * gain_time_ref[...]).astype(BF16)
     queries = dot(normed_half, query_time_ref[...]).astype(BF16)
     keys = dot(normed_half, key_time_ref[...]).astype(BF16)
-    copies[0].wait()
-    values = dot(normed_half, value_time_ref[...]).astype(BF16)
-    qkv = jnp.concatenate([queries, keys, values], axis=1)
-    qkv_ref[...] = qkv
-    copies[1].wait()
-    grad_out = dot_last(cotangent, out_space_ref[...]).astype(BF16)
-    qkv_t = qkv.T
-    queries_t = qkv_t[:features] * jnp.asarray(size ** -0.5, BF16)
+    qkv_ref[:, :features] = queries
+    qkv_ref[:, features : 2 * features] = keys
+    queries_t = queries.T * jnp.asarray(size ** -0.5, BF16)
     rows = lax.broadcasted_iota(jnp.int32, (tokens, tokens), 0)
     columns = lax.broadcasted_iota(jnp.int32, (tokens, tokens), 1)
     bias = jnp.where((rows % patches) == (columns % patches), 0.0, -1e30)
     ones = jnp.ones((16, tokens), BF16)
 
     def attention(h):
-        keys = qkv[:, features + h * size : features + (h + 1) * size]
-        scores = dot(keys, queries_t[h * size : (h + 1) * size]) + bias
+        own = slice(h * size, (h + 1) * size)
+        scores = dot(keys[:, own], queries_t[own]) + bias
         yield
         weights = jnp.exp(scores - jnp.max(scores, axis=0, keepdims=True)).astype(BF16)
         weights_ref[h] = weights
         yield
-        values_t = qkv_t[2 * features + h * size : 2 * features + (h + 1) * size]
-        sums = dot(jnp.concatenate([values_t, ones], axis=0), weights)
+        sums = dot(jnp.concatenate([values_t[own], ones], axis=0), weights)
         inverse = 1.0 / sums[size : size + 1]
         inverse_ref[h : h + 1] = inverse
-        return sums[:size] * inverse
-
-    outputs = []
-    for h in range(0, HEADS, together):
+        return (sums[:size] * inverse).astype(BF16)
+
+    first = [attention(h) for h in range(together)]
+    for one in first:
+        next(one)
+    copies[0].wait()
+    copies[1].wait()
+    values = dot(normed_half, value_time_ref[...]).astype(BF16)
+    qkv_ref[:, 2 * features :] = values
+    values_t = values.T
+    grad_out = dot_last(cotangent, out_space_ref[...]).astype(BF16)
+    outputs = in_turn(first)
+    for h in range(together, HEADS, together):
         outputs += in_turn(attention(h + n) for n in range(together))
-    attended = jnp.concatenate(outputs, axis=0).T.astype(BF16)
+    attended = jnp.concatenate(outputs, axis=0).T
     attended_ref[...] = attended
     copies[2].wait()
     hidden = (tokens_in + dot(attended, out_time_ref[...])).astype(BF16)
@@ -156,13 +159,11 @@
             tra[n, h, :size] = piece * jnp.asarray(scale, BF16) if n == 0 else piece
             if n == 2:
                 tra[n, h, size:] = jnp.ones((tra.shape[2] - size, tokens), BF16)
-    grad_key[...] = jnp.zeros_like(grad_key)
-    grad_value[...] = jnp.zeros_like(grad_value)
     blocks = tokens // block
 
     def attention(t):
         h = t // blocks
-        here = pl.ds(pl.multiple_of(t % blocks * block, block), block)
+        here = pl.ds(t % blocks * block, block)
         query_t = tra[0, h, :size, here]
         grad_out_t = tra[3, h, :size, here]
         scores = dot(nat[0, h], query_t)
@@ -177,18 +178,20 @@
         grad_prob = dot(nat[1, h], grad_out_t)
         grad_scores = (weights.astype(F32) * (grad_prob - delta)).astype(BF16)
         yield
-        grad_t[h, :, here] = dot(tra[1, h, :size], grad_scores) * (inverse * scale)
-        grad_key[h] += dot_last(grad_scores, (query_t.astype(F32) * inverse).astype(BF16))
-        grad_value[h] += dot_last(weights, (grad_out_t.astype(F32) * inverse).astype(BF16))
-
-    def step(t, carry):
-        in_turn(attention(t * together + n) for n in range(together))
-        return carry
-
-    lax.fori_loop(0, heads * blocks // together, step, 0)
+        grad_t[h, :, here] = (dot(tra[1, h, :size], grad_scores) * (inverse * scale)).astype(BF16)
+        key_terms = dot_last(grad_scores, (query_t.astype(F32) * inverse).astype(BF16))
+        value_terms = dot_last(weights, (grad_out_t.astype(F32) * inverse).astype(BF16))
+        if t % blocks == 0:
+            grad_key[h], grad_value[h] = key_terms, value_terms
+        else:
+            grad_key[h] += key_terms
+            grad_value[h] += value_terms
+
+    for t in range(0, heads * blocks, together):
+        in_turn(attention(t + n) for n in range(together))
     back_ref[:, : part * 2] = jnp.concatenate(
-        [out_t[h].astype(F32) for h in range(heads)] + [grad_t[h] for h in range(heads)], axis=0
-    ).T.astype(BF16)
+        [out_t[h] for h in range(heads)] + [grad_t[h] for h in range(heads)], axis=0
+    ).T
     back_ref[:, part * 2 :] = jnp.concatenate(
         [grad_key[h] for h in range(heads)] + [grad_value[h] for h in range(heads)], axis=1
     ).astype(BF16)
@@ -328,7 +331,7 @@
     rows = devices * own_patches
     size = features // HEADS
     back = pl.pallas_call(
-        functools.partial(space_kernel, heads, 256, 12),
+        functools.partial(space_kernel, heads, 256, 4),
         out_shape=shaped((rows, 4 * part)),
         in_specs=[VMEM],
         out_specs=VMEM,
@@ -336,7 +339,7 @@
             pltpu.VMEM((2, heads, rows, size), BF16),
             pltpu.VMEM((4, heads, size + 16, rows), BF16),
             pltpu.VMEM((heads, size, rows), BF16),
-            pltpu.VMEM((heads, size, rows), F32),
+            pltpu.VMEM((heads, size, rows), BF16),
             pltpu.VMEM((heads, rows, size), F32),
             pltpu.VMEM((heads, rows, size), F32),
         ],

time: 122 us -> 121 us (level)
  no operation moved by 1% of the time
where the time goes in v4:
time: 121 us
  blocking collectives  75.8 us (63%)
  Pallas kernels  23.7 us (20%)
  waiting for transfers between devices  11.2 us (9%)
  starting transfers between devices  6.41 us (5%)
  other arithmetic  2.09 us (2%)
    all_to_all x1, blocking collectives, local(): lax.all_to_all(send.reshape(devices, own_patches, 4 * part), ('frame', 't...  31.8 us
    all_to_all x1, blocking collectives, local(): lax.all_to_all(back.reshape(devices, own_patches, 4 * part), ('frame', 't...  28.8 us
    all_to_all x1, blocking collectives, local(): result = lax.all_to_all(result, 'frame', 0, 0)  15.2 us
    all_to_all x1, waiting for transfers between devices, local(): both = lax.all_to_all(both, 'frame', 0, 0)  11.2 us
    pallas_call x1, Pallas kernels, local(): pl.pallas_call(functools.partial(space_kernel, heads, 256, 4), out_shape=...  10.7 us
    all_to_all x1, starting transfers between devices, local(): both = lax.all_to_all(both, 'frame', 0, 0)  6.41 us
    pallas_call x1, Pallas kernels, local(): pl.pallas_call(functools.partial(time_backward_kernel, 6), out_shape=shap...  5.86 us
    pallas_call x1, Pallas kernels, local(): pl.pallas_call(functools.partial(time_forward_kernel, own_patches, groups...  5.46 us
  transfers between devices with their start and end apart: 1, of which 1 were waited for; matrix products, arithmetic and copies ran while one was open for 0% of the time, Pallas kernels for 1%

profile of v4, /device:TPU:0, one launch (start us, length us, event | category | flops | bytes accessed | tf_op | source)
XLA Modules:
  0.0 121.0 jit_solution(942074397873164067)
XLA Ops:
  0.6 2.1 %copy_bitcast_fusion = bf16[8,2,4,8,768]{4,3,2,1,0:T(8,128)(2,1)} fusion(bf16[1,4,8,8,768]{4,3,2,1,0:T(8,128)(2,1)} %bitcast.23, bf16[1,4,8,8,768]{4,3,2,1,0:T(8,128)(2,1)} %bitcast.24), kind=kLoop, calls=%fused_computation.1 | loop fusion | flops 393216 | bytes 1572864 | tf_op jit(solution)/shard_map/transpose | solution.py:300
  2.7 6.4 %all-to-all-start = ((bf16[8,2,4,8,768]{4,3,2,1,0:T(8,128)(2,1)}), bf16[8,2,4,8,768]{4,3,2,1,0:T(8,128)(2,1)S(1)}, u32[]{:S(2)}, u32[]{:S(2)}) async-start(bf16[8,2,4,8,768]{4,3,2,1,0:T(8,128)(2,1)} %copy_bitcast_fusion), calls=%async_computation | async-start | bytes 1572864 | tf_op jit(solution)/shard_map/all_to_all | solution.py:301
  9.1 0.0 copy-start.4
  9.1 0.0 copy-start.5
  9.1 1.7 %fetch_weights.1 = (bf16[768,768]{1,0:T(8,128)(2,1)S(1)}, bf16[768,768]{1,0:T(8,128)(2,1)S(1)}) custom-call(bf16[768,2304]{1,0:T(8,128)(2,1)} %qkv_time_ref.1), custom_call_target="tpu_custom_call" | custom-call | bytes 20971520 | tf_op jit(solution)/shard_map/fetch_weights/pallas_call | solution.py:288
  10.8 11.2 %all-to-all-done = bf16[8,2,4,8,768]{4,3,2,1,0:T(8,128)(2,1)S(1)} async-done(((bf16[8,2,4,8,768]{4,3,2,1,0:T(8,128)(2,1)}), bf16[8,2,4,8,768]{4,3,2,1,0:T(8,128)(2,1)S(1)}, u32[]{:S(2)}, u32[]{:S(2)}) %all-to-all-start) | async-done | bytes 786464 | tf_op jit(solution)/shard_map/all_to_all | solution.py:301
  22.0 0.0 copy-done.4
  22.0 0.0 copy-done.5
  22.0 5.5 %time_forward.1 = (bf16[4,256,768]{2,1,0:T(8,128)(2,1)S(1)}, bf16[256,768]{1,0:T(8,128)(2,1)S(1)}, bf16[256,2304]{1,0:T(8,128)(2,1)S(1)}, bf16[256,768]{1,0:T(8,...) custom-call(bf16[8,2,32,768]{3,2,1,0:T(8,128)(2,1)S(1)} %bitcast.16, f32[768]{0:T(1024)S(1)} %copy-done.4, ...), custom_call_target="tpu_custom_call" | custom-call | tf_op jit(solution)/shard_map/time_forward/pallas_call | solution.py:304
  27.5 0.0 copy-start.1
  27.5 31.8 %all_to_all.20 = bf16[128,8,768]{2,1,0:T(8,128)(2,1)S(1)} all-to-all(bf16[128,8,768]{2,1,0:T(8,128)(2,1)S(1)} %bitcast.21), channel_id=1, replica_groups=mesh['frame'=8,'tile'=16] {'frame','tile'}, dimensions={0} | all-to-all | bytes 3145728 | tf_op jit(solution)/shard_map/all_to_all | solution.py:327
  59.3 0.0 copy-start
  59.3 10.7 %space_attention.1 = bf16[1024,768]{1,0:T(8,128)(2,1)S(1)} custom-call(bf16[1024,768]{1,0:T(8,128)(2,1)S(1)} %bitcast.19), custom_call_target="tpu_custom_call" | custom-call | tf_op jit(solution)/shard_map/space_attention/pallas_call | solution.py:333
  70.0 0.0 copy-start.2
  70.1 0.0 copy-start.3
  70.1 28.8 %all_to_all.21 = bf16[128,8,768]{2,1,0:T(8,128)(2,1)S(1)} all-to-all(bf16[128,8,768]{2,1,0:T(8,128)(2,1)S(1)} %bitcast.20), channel_id=1, replica_groups=mesh['frame'=8,'tile'=16] {'frame','tile'}, dimensions={0} | all-to-all | bytes 3145728 | tf_op jit(solution)/shard_map/all_to_all | solution.py:350
  98.9 0.0 copy-done.1
  98.9 0.0 copy-done
  98.9 0.0 copy-done.2
  98.9 0.0 copy-done.3
  98.9 5.9 %time_backward.1 = bf16[8,2,32,768]{3,2,1,0:T(8,128)(2,1)S(1)} custom-call(bf16[8,2,32,768]{3,2,1,0:T(8,128)(2,1)S(1)} %bitcast.17, bf16[4,256,768]{2,1,0:T(8,128)(2,1)S(1)} %bitcast.18, bf16[256,768]{1,0:T(8,128)(2,1)S(1)} %get-tuple-element.13.hidden_ref, bf16[256,2304]{1,0:T(8,128)(2,1)S(1)} %get-tuple-element.14.qkv_ref, ...), custom_call_target="tpu_custom_call" | custom-call | tf_op jit(solution)/shard_map/time_backward/pallas_call | solution.py:354
  104.8 15.2 %all_to_all.22 = bf16[8,2,32,768]{3,2,1,0:T(8,128)(2,1)S(1)} all-to-all(bf16[8,2,32,768]{3,2,1,0:T(8,128)(2,1)S(1)} %time_backward.1), channel_id=1, replica_groups=mesh['frame'=8,'tile'=16] {'frame'}, dimensions={0} | all-to-all | bytes 1572864 | tf_op jit(solution)/shard_map/all_to_all | solution.py:363
  120.0 0.1 fusion
  120.0 0.9 copy_bitcast_fusion.1
Async XLA Ops:
  2.7 19.3 %all-to-all-start = ((bf16[8,2,4,8,768]{4,3,2,1,0:T(8,128)(2,1)}), bf16[8,2,4,8,768]{4,3,2,1,0:T(8,128)(2,1)S(1)}, u32[]{:S(2)}, u32[]{:S(2)}) async-start(bf16[8,2,4,8,768]{4,3,2,1,0:T(8,128)(2,1)} %copy_bitcast_fusion), calls=%async_computation | async-start | bytes 1572864 | tf_op jit(solution)/shard_map/all_to_all | solution.py:301
  9.1 12.9 %copy-start.4 = (f32[768]{0:T(1024)S(1)}, f32[768]{0:T(1024)}, u32[]{:S(2)}) copy-start(f32[768]{0:T(1024)} %gain_time_ref.3) | copy-start | bytes 9220
  9.1 12.9 %copy-start.5 = (f32[768]{0:T(1024)S(1)}, f32[768]{0:T(1024)}, u32[]{:S(2)}) copy-start(f32[768]{0:T(1024)} %gain_space_ref.3) | copy-start | bytes 9220
  27.5 71.4 %copy-start.1 = (bf16[768,2304]{1,0:T(8,128)(2,1)S(1)}, bf16[768,2304]{1,0:T(8,128)(2,1)}, u32[]{:S(2)}) copy-start(bf16[768,2304]{1,0:T(8,128)(2,1)} %qkv_space_ref.1) | copy-start | bytes 10616836
  59.3 39.6 %copy-start = (bf16[768,2304]{1,0:T(8,128)(2,1)S(1)}, bf16[768,2304]{1,0:T(8,128)(2,1)}, u32[]{:S(2)}) copy-start(bf16[768,2304]{1,0:T(8,128)(2,1)} %qkv_time_ref.1) | copy-start | bytes 10616836
  70.0 28.9 %copy-start.2 = (bf16[768,768]{1,0:T(8,128)(2,1)S(1)}, bf16[768,768]{1,0:T(8,128)(2,1)}, u32[]{:S(2)}) copy-start(bf16[768,768]{1,0:T(8,128)(2,1)} %out_time_ref.1) | copy-start | bytes 3538948
  70.1 28.9 %copy-start.3 = (bf16[768,768]{1,0:T(8,128)(2,1)S(1)}, bf16[768,768]{1,0:T(8,128)(2,1)}, u32[]{:S(2)}) copy-start(bf16[768,768]{1,0:T(8,128)(2,1)} %out_space_ref.1) | copy-start | bytes 3538948

commit v5 on v4

--- a/solution.py
+++ b/solution.py
@@ -120,7 +120,7 @@
     values = dot(normed_half, value_time_ref[...]).astype(BF16)
     qkv_ref[:, 2 * features :] = values
     values_t = values.T
-    grad_out = dot_last(cotangent, out_space_ref[...]).astype(BF16)
+    grad_out = dot_last(out_space_ref[...], cotangent).astype(BF16).T
     outputs = in_turn(first)
     for h in range(together, HEADS, together):
         outputs += in_turn(attention(h + n) for n in range(together))
@@ -224,11 +224,10 @@
     grad_hidden = (
         cotangent + norm_backward(grad_normed, gain_space_ref[...], normed, inverse)
     ).astype(BF16)
-    grad_out = dot_last(grad_hidden, out_time_ref[...]).astype(BF16)
+    grad_out_t = dot_last(out_time_ref[...], grad_hidden).astype(BF16)
     qkv = qkv_ref[...]
     keys_t = qkv[:, features : 2 * features].T
-    grad_out_t = grad_out.T
-    product_t = (grad_out.astype(F32) * attended_ref[...].astype(F32)).T
+    product_t = grad_out_t.astype(F32) * attended_ref[...].T.astype(F32)
     queries_t = qkv[:, :features].T
 
     def attention(h):
@@ -252,7 +251,7 @@
     queries_grad, keys_grad, values_grad = zip(*ended)
     grad_qkv_time = jnp.concatenate(
         [
-            jnp.concatenate(queries_grad, axis=0).T.astype(BF16),
+            jnp.concatenate([g.astype(BF16) for g in queries_grad], axis=0).T,
             jnp.concatenate(keys_grad, axis=1).astype(BF16),
             jnp.concatenate(values_grad, axis=1).astype(BF16),
         ],

time: 121 us -> 121 us (level)
  no operation moved by 1% of the time
where the time goes in v5:
time: 121 us; the launch traced here: 120 us
  blocking collectives  75.8 us (63%)
  Pallas kernels  23.1 us (19%)
  waiting for transfers between devices  11.2 us (9%)
  starting transfers between devices  6.41 us (5%)
  other arithmetic  2.09 us (2%)
    all_to_all x1, blocking collectives, local(): lax.all_to_all(send.reshape(devices, own_patches, 4 * part), ('frame', 't...  31.8 us
    all_to_all x1, blocking collectives, local(): lax.all_to_all(back.reshape(devices, own_patches, 4 * part), ('frame', 't...  28.8 us
    all_to_all x1, blocking collectives, local(): result = lax.all_to_all(result, 'frame', 0, 0)  15.2 us
    all_to_all x1, waiting for transfers between devices, local(): both = lax.all_to_all(both, 'frame', 0, 0)  11.2 us
    pallas_call x1, Pallas kernels, local(): pl.pallas_call(functools.partial(space_kernel, heads, 256, 4), out_shape=...  10.7 us
    all_to_all x1, starting transfers between devices, local(): both = lax.all_to_all(both, 'frame', 0, 0)  6.41 us
    pallas_call x1, Pallas kernels, local(): pl.pallas_call(functools.partial(time_backward_kernel, 6), out_shape=shap...  5.45 us
    pallas_call x1, Pallas kernels, local(): pl.pallas_call(functools.partial(time_forward_kernel, own_patches, groups...  5.32 us
  transfers between devices with their start and end apart: 1, of which 1 were waited for; matrix products, arithmetic and copies ran while one was open for 0% of the time, Pallas kernels for 1%

profile of v5, /device:TPU:0, one launch (start us, length us, event | category | flops | bytes accessed | tf_op | source)
XLA Modules:
  0.0 120.4 jit_solution(16385454485606568355)
XLA Ops:
  0.6 2.1 %copy_bitcast_fusion = bf16[8,2,4,8,768]{4,3,2,1,0:T(8,128)(2,1)} fusion(bf16[1,4,8,8,768]{4,3,2,1,0:T(8,128)(2,1)} %bitcast.23, bf16[1,4,8,8,768]{4,3,2,1,0:T(8,128)(2,1)} %bitcast.24), kind=kLoop, calls=%fused_computation.1 | loop fusion | flops 393216 | bytes 1572864 | tf_op jit(solution)/shard_map/transpose | solution.py:299
  2.7 6.4 %all-to-all-start = ((bf16[8,2,4,8,768]{4,3,2,1,0:T(8,128)(2,1)}), bf16[8,2,4,8,768]{4,3,2,1,0:T(8,128)(2,1)S(1)}, u32[]{:S(2)}, u32[]{:S(2)}) async-start(bf16[8,2,4,8,768]{4,3,2,1,0:T(8,128)(2,1)} %copy_bitcast_fusion), calls=%async_computation | async-start | bytes 1572864 | tf_op jit(solution)/shard_map/all_to_all | solution.py:300
  9.1 0.0 copy-start.4
  9.1 0.0 copy-start.5
  9.1 1.7 %fetch_weights.1 = (bf16[768,768]{1,0:T(8,128)(2,1)S(1)}, bf16[768,768]{1,0:T(8,128)(2,1)S(1)}) custom-call(bf16[768,2304]{1,0:T(8,128)(2,1)} %qkv_time_ref.1), custom_call_target="tpu_custom_call" | custom-call | bytes 20971520 | tf_op jit(solution)/shard_map/fetch_weights/pallas_call | solution.py:287
  10.8 11.2 %all-to-all-done = bf16[8,2,4,8,768]{4,3,2,1,0:T(8,128)(2,1)S(1)} async-done(((bf16[8,2,4,8,768]{4,3,2,1,0:T(8,128)(2,1)}), bf16[8,2,4,8,768]{4,3,2,1,0:T(8,128)(2,1)S(1)}, u32[]{:S(2)}, u32[]{:S(2)}) %all-to-all-start) | async-done | bytes 786464 | tf_op jit(solution)/shard_map/all_to_all | solution.py:300
  22.0 0.0 copy-done.4
  22.0 0.0 copy-done.5
  22.0 5.3 %time_forward.1 = (bf16[4,256,768]{2,1,0:T(8,128)(2,1)S(1)}, bf16[256,768]{1,0:T(8,128)(2,1)S(1)}, bf16[256,2304]{1,0:T(8,128)(2,1)S(1)}, bf16[256,768]{1,0:T(8,...) custom-call(bf16[8,2,32,768]{3,2,1,0:T(8,128)(2,1)S(1)} %bitcast.16, f32[768]{0:T(1024)S(1)} %copy-done.4, ...), custom_call_target="tpu_custom_call" | custom-call | tf_op jit(solution)/shard_map/time_forward/pallas_call | solution.py:303
  27.3 0.0 copy-start.1
  27.4 31.8 %all_to_all.20 = bf16[128,8,768]{2,1,0:T(8,128)(2,1)S(1)} all-to-all(bf16[128,8,768]{2,1,0:T(8,128)(2,1)S(1)} %bitcast.21), channel_id=1, replica_groups=mesh['frame'=8,'tile'=16] {'frame','tile'}, dimensions={0} | all-to-all | bytes 3145728 | tf_op jit(solution)/shard_map/all_to_all | solution.py:326
  59.2 0.0 copy-start
  59.2 10.7 %space_attention.1 = bf16[1024,768]{1,0:T(8,128)(2,1)S(1)} custom-call(bf16[1024,768]{1,0:T(8,128)(2,1)S(1)} %bitcast.19), custom_call_target="tpu_custom_call" | custom-call | tf_op jit(solution)/shard_map/space_attention/pallas_call | solution.py:332
  69.9 0.0 copy-start.2
  69.9 0.0 copy-start.3
  69.9 28.8 %all_to_all.21 = bf16[128,8,768]{2,1,0:T(8,128)(2,1)S(1)} all-to-all(bf16[128,8,768]{2,1,0:T(8,128)(2,1)S(1)} %bitcast.20), channel_id=1, replica_groups=mesh['frame'=8,'tile'=16] {'frame','tile'}, dimensions={0} | all-to-all | bytes 3145728 | tf_op jit(solution)/shard_map/all_to_all | solution.py:349
  98.8 0.0 copy-done.1
  98.8 0.0 copy-done
  98.8 0.0 copy-done.2
  98.8 0.0 copy-done.3
  98.8 5.4 %time_backward.1 = bf16[8,2,32,768]{3,2,1,0:T(8,128)(2,1)S(1)} custom-call(bf16[8,2,32,768]{3,2,1,0:T(8,128)(2,1)S(1)} %bitcast.17, bf16[4,256,768]{2,1,0:T(8,128)(2,1)S(1)} %bitcast.18, bf16[256,768]{1,0:T(8,128)(2,1)S(1)} %get-tuple-element.13.hidden_ref, bf16[256,2304]{1,0:T(8,128)(2,1)S(1)} %get-tuple-element.14.qkv_ref, ...), custom_call_target="tpu_custom_call" | custom-call | tf_op jit(solution)/shard_map/time_backward/pallas_call | solution.py:353
  104.2 15.2 %all_to_all.22 = bf16[8,2,32,768]{3,2,1,0:T(8,128)(2,1)S(1)} all-to-all(bf16[8,2,32,768]{3,2,1,0:T(8,128)(2,1)S(1)} %time_backward.1), channel_id=1, replica_groups=mesh['frame'=8,'tile'=16] {'frame'}, dimensions={0} | all-to-all | bytes 1572864 | tf_op jit(solution)/shard_map/all_to_all | solution.py:362
  119.4 0.1 fusion
  119.5 0.9 copy_bitcast_fusion.1
Async XLA Ops:
  2.7 19.3 %all-to-all-start = ((bf16[8,2,4,8,768]{4,3,2,1,0:T(8,128)(2,1)}), bf16[8,2,4,8,768]{4,3,2,1,0:T(8,128)(2,1)S(1)}, u32[]{:S(2)}, u32[]{:S(2)}) async-start(bf16[8,2,4,8,768]{4,3,2,1,0:T(8,128)(2,1)} %copy_bitcast_fusion), calls=%async_computation | async-start | bytes 1572864 | tf_op jit(solution)/shard_map/all_to_all | solution.py:300
  9.1 12.9 %copy-start.4 = (f32[768]{0:T(1024)S(1)}, f32[768]{0:T(1024)}, u32[]{:S(2)}) copy-start(f32[768]{0:T(1024)} %gain_time_ref.3) | copy-start | bytes 9220
  9.1 12.9 %copy-start.5 = (f32[768]{0:T(1024)S(1)}, f32[768]{0:T(1024)}, u32[]{:S(2)}) copy-start(f32[768]{0:T(1024)} %gain_space_ref.3) | copy-start | bytes 9220
  27.3 71.4 %copy-start.1 = (bf16[768,2304]{1,0:T(8,128)(2,1)S(1)}, bf16[768,2304]{1,0:T(8,128)(2,1)}, u32[]{:S(2)}) copy-start(bf16[768,2304]{1,0:T(8,128)(2,1)} %qkv_space_ref.1) | copy-start | bytes 10616836
  59.2 39.6 %copy-start = (bf16[768,2304]{1,0:T(8,128)(2,1)S(1)}, bf16[768,2304]{1,0:T(8,128)(2,1)}, u32[]{:S(2)}) copy-start(bf16[768,2304]{1,0:T(8,128)(2,1)} %qkv_time_ref.1) | copy-start | bytes 10616836
  69.9 28.9 %copy-start.2 = (bf16[768,768]{1,0:T(8,128)(2,1)S(1)}, bf16[768,768]{1,0:T(8,128)(2,1)}, u32[]{:S(2)}) copy-start(bf16[768,768]{1,0:T(8,128)(2,1)} %out_time_ref.1) | copy-start | bytes 3538948
  69.9 28.9 %copy-start.3 = (bf16[768,768]{1,0:T(8,128)(2,1)S(1)}, bf16[768,768]{1,0:T(8,128)(2,1)}, u32[]{:S(2)}) copy-start(bf16[768,768]{1,0:T(8,128)(2,1)} %out_space_ref.1) | copy-start | bytes 3538948

commit v6 on v5

--- a/solution.py
+++ b/solution.py
@@ -301,7 +301,7 @@
     both = both.reshape(frame_count, 2, frames * own_patches, features)
 
     send, hidden, qkv, attended, scores, inverse = pl.pallas_call(
-        functools.partial(time_forward_kernel, own_patches, groups, 6),
+        functools.partial(time_forward_kernel, own_patches, groups, 12),
         out_shape=(
             shaped((groups, tokens, 4 * part)),
             shaped((tokens, features)),

time: 121 us -> 120 us (level)
  no operation moved by 1% of the time
where the time goes in v6:
time: 120 us
  blocking collectives  75.8 us (63%)
  Pallas kernels  22.9 us (19%)
  waiting for transfers between devices  11.2 us (9%)
  starting transfers between devices  6.41 us (5%)
  other arithmetic  2.09 us (2%)
    all_to_all x1, blocking collectives, local(): lax.all_to_all(send.reshape(devices, own_patches, 4 * part), ('frame', 't...  31.8 us
    all_to_all x1, blocking collectives, local(): lax.all_to_all(back.reshape(devices, own_patches, 4 * part), ('frame', 't...  28.8 us
    all_to_all x1, blocking collectives, local(): result = lax.all_to_all(result, 'frame', 0, 0)  15.2 us
    all_to_all x1, waiting for transfers between devices, local(): both = lax.all_to_all(both, 'frame', 0, 0)  11.2 us
    pallas_call x1, Pallas kernels, local(): pl.pallas_call(functools.partial(space_kernel, heads, 256, 4), out_shape=...  10.7 us
    all_to_all x1, starting transfers between devices, local(): both = lax.all_to_all(both, 'frame', 0, 0)  6.41 us
    pallas_call x1, Pallas kernels, local(): pl.pallas_call(functools.partial(time_backward_kernel, 6), out_shape=shap...  5.45 us
    pallas_call x1, Pallas kernels, local(): pl.pallas_call(functools.partial(time_forward_kernel, own_patches, groups...  5 us
  transfers between devices with their start and end apart: 1, of which 1 were waited for; matrix products, arithmetic and copies ran while one was open for 0% of the time, Pallas kernels for 1%

profile of v6, /device:TPU:0, one launch (start us, length us, event | category | flops | bytes accessed | tf_op | source)
XLA Modules:
  0.0 120.1 jit_solution(1844331545450406529)
XLA Ops:
  0.6 2.1 %copy_bitcast_fusion = bf16[8,2,4,8,768]{4,3,2,1,0:T(8,128)(2,1)} fusion(bf16[1,4,8,8,768]{4,3,2,1,0:T(8,128)(2,1)} %bitcast.23, bf16[1,4,8,8,768]{4,3,2,1,0:T(8,128)(2,1)} %bitcast.24), kind=kLoop, calls=%fused_computation.1 | loop fusion | flops 393216 | bytes 1572864 | tf_op jit(solution)/shard_map/transpose | solution.py:299
  2.7 6.4 %all-to-all-start = ((bf16[8,2,4,8,768]{4,3,2,1,0:T(8,128)(2,1)}), bf16[8,2,4,8,768]{4,3,2,1,0:T(8,128)(2,1)S(1)}, u32[]{:S(2)}, u32[]{:S(2)}) async-start(bf16[8,2,4,8,768]{4,3,2,1,0:T(8,128)(2,1)} %copy_bitcast_fusion), calls=%async_computation | async-start | bytes 1572864 | tf_op jit(solution)/shard_map/all_to_all | solution.py:300
  9.1 0.0 copy-start.4
  9.1 0.0 copy-start.5
  9.1 1.7 %fetch_weights.1 = (bf16[768,768]{1,0:T(8,128)(2,1)S(1)}, bf16[768,768]{1,0:T(8,128)(2,1)S(1)}) custom-call(bf16[768,2304]{1,0:T(8,128)(2,1)} %qkv_time_ref.1), custom_call_target="tpu_custom_call" | custom-call | bytes 20971520 | tf_op jit(solution)/shard_map/fetch_weights/pallas_call | solution.py:287
  10.8 11.2 %all-to-all-done = bf16[8,2,4,8,768]{4,3,2,1,0:T(8,128)(2,1)S(1)} async-done(((bf16[8,2,4,8,768]{4,3,2,1,0:T(8,128)(2,1)}), bf16[8,2,4,8,768]{4,3,2,1,0:T(8,128)(2,1)S(1)}, u32[]{:S(2)}, u32[]{:S(2)}) %all-to-all-start) | async-done | bytes 786464 | tf_op jit(solution)/shard_map/all_to_all | solution.py:300
  22.0 0.0 copy-done.4
  22.0 0.0 copy-done.5
  22.0 5.0 %time_forward.1 = (bf16[4,256,768]{2,1,0:T(8,128)(2,1)S(1)}, bf16[256,768]{1,0:T(8,128)(2,1)S(1)}, bf16[256,2304]{1,0:T(8,128)(2,1)S(1)}, bf16[256,768]{1,0:T(8,...) custom-call(bf16[8,2,32,768]{3,2,1,0:T(8,128)(2,1)S(1)} %bitcast.16, f32[768]{0:T(1024)S(1)} %copy-done.4, ...), custom_call_target="tpu_custom_call" | custom-call | tf_op jit(solution)/shard_map/time_forward/pallas_call | solution.py:303
  27.0 0.0 copy-start.1
  27.0 31.8 %all_to_all.20 = bf16[128,8,768]{2,1,0:T(8,128)(2,1)S(1)} all-to-all(bf16[128,8,768]{2,1,0:T(8,128)(2,1)S(1)} %bitcast.21), channel_id=1, replica_groups=mesh['frame'=8,'tile'=16] {'frame','tile'}, dimensions={0} | all-to-all | bytes 3145728 | tf_op jit(solution)/shard_map/all_to_all | solution.py:326
  58.9 0.0 copy-start
  58.9 10.7 %space_attention.1 = bf16[1024,768]{1,0:T(8,128)(2,1)S(1)} custom-call(bf16[1024,768]{1,0:T(8,128)(2,1)S(1)} %bitcast.19), custom_call_target="tpu_custom_call" | custom-call | tf_op jit(solution)/shard_map/space_attention/pallas_call | solution.py:332
  69.6 0.0 copy-start.2
  69.6 0.0 copy-start.3
  69.6 28.8 %all_to_all.21 = bf16[128,8,768]{2,1,0:T(8,128)(2,1)S(1)} all-to-all(bf16[128,8,768]{2,1,0:T(8,128)(2,1)S(1)} %bitcast.20), channel_id=1, replica_groups=mesh['frame'=8,'tile'=16] {'frame','tile'}, dimensions={0} | all-to-all | bytes 3145728 | tf_op jit(solution)/shard_map/all_to_all | solution.py:349
  98.5 0.0 copy-done.1
  98.5 0.0 copy-done
  98.5 0.0 copy-done.2
  98.5 0.0 copy-done.3
  98.5 5.5 %time_backward.1 = bf16[8,2,32,768]{3,2,1,0:T(8,128)(2,1)S(1)} custom-call(bf16[8,2,32,768]{3,2,1,0:T(8,128)(2,1)S(1)} %bitcast.17, bf16[4,256,768]{2,1,0:T(8,128)(2,1)S(1)} %bitcast.18, bf16[256,768]{1,0:T(8,128)(2,1)S(1)} %get-tuple-element.13.hidden_ref, bf16[256,2304]{1,0:T(8,128)(2,1)S(1)} %get-tuple-element.14.qkv_ref, ...), custom_call_target="tpu_custom_call" | custom-call | tf_op jit(solution)/shard_map/time_backward/pallas_call | solution.py:353
  104.0 15.2 %all_to_all.22 = bf16[8,2,32,768]{3,2,1,0:T(8,128)(2,1)S(1)} all-to-all(bf16[8,2,32,768]{3,2,1,0:T(8,128)(2,1)S(1)} %time_backward.1), channel_id=1, replica_groups=mesh['frame'=8,'tile'=16] {'frame'}, dimensions={0} | all-to-all | bytes 1572864 | tf_op jit(solution)/shard_map/all_to_all | solution.py:362
  119.1 0.1 fusion
  119.2 0.9 copy_bitcast_fusion.1
Async XLA Ops:
  2.7 19.3 %all-to-all-start = ((bf16[8,2,4,8,768]{4,3,2,1,0:T(8,128)(2,1)}), bf16[8,2,4,8,768]{4,3,2,1,0:T(8,128)(2,1)S(1)}, u32[]{:S(2)}, u32[]{:S(2)}) async-start(bf16[8,2,4,8,768]{4,3,2,1,0:T(8,128)(2,1)} %copy_bitcast_fusion), calls=%async_computation | async-start | bytes 1572864 | tf_op jit(solution)/shard_map/all_to_all | solution.py:300
  9.1 12.9 %copy-start.4 = (f32[768]{0:T(1024)S(1)}, f32[768]{0:T(1024)}, u32[]{:S(2)}) copy-start(f32[768]{0:T(1024)} %gain_time_ref.3) | copy-start | bytes 9220
  9.1 12.9 %copy-start.5 = (f32[768]{0:T(1024)S(1)}, f32[768]{0:T(1024)}, u32[]{:S(2)}) copy-start(f32[768]{0:T(1024)} %gain_space_ref.3) | copy-start | bytes 9220
  27.0 71.5 %copy-start.1 = (bf16[768,2304]{1,0:T(8,128)(2,1)S(1)}, bf16[768,2304]{1,0:T(8,128)(2,1)}, u32[]{:S(2)}) copy-start(bf16[768,2304]{1,0:T(8,128)(2,1)} %qkv_space_ref.1) | copy-start | bytes 10616836
  58.9 39.6 %copy-start = (bf16[768,2304]{1,0:T(8,128)(2,1)S(1)}, bf16[768,2304]{1,0:T(8,128)(2,1)}, u32[]{:S(2)}) copy-start(bf16[768,2304]{1,0:T(8,128)(2,1)} %qkv_time_ref.1) | copy-start | bytes 10616836
  69.6 28.9 %copy-start.2 = (bf16[768,768]{1,0:T(8,128)(2,1)S(1)}, bf16[768,768]{1,0:T(8,128)(2,1)}, u32[]{:S(2)}) copy-start(bf16[768,768]{1,0:T(8,128)(2,1)} %out_time_ref.1) | copy-start | bytes 3538948
  69.6 28.9 %copy-start.3 = (bf16[768,768]{1,0:T(8,128)(2,1)S(1)}, bf16[768,768]{1,0:T(8,128)(2,1)}, u32[]{:S(2)}) copy-start(bf16[768,768]{1,0:T(8,128)(2,1)} %out_space_ref.1) | copy-start | bytes 3538948
